TPU v7x, 1024 devices: a whole 8x8x8 slice. The times are simulated.
1024 devices in a mesh: dp: 64 (over y_hi, x, core), expert: 16 (over z, y_lo).
Axes of the slice: x: 8, y: 8 (y_hi: 4, y_lo: 2; y = y_hi * 2 + y_lo), z: 8, core: 2. Of those that a mesh axis runs over, the one named last changes fastest.
Arguments:
- token_values: bfloat16 [131072, 3584], P(('dp', 'expert')), may hold values from -24 to 24
- block_scales: bfloat16 [131072, 28], P(('dp', 'expert')), may hold values from 0.25 to 4
- route_ids: int32 [131072, 8], P(('dp', 'expert')), may hold values from 0 to 255, as said below
- route_slots: int32 [131072], P(('dp', 'expert')), may hold values from 0 to 127, as said below
- router_logits: float32 [131072, 256], P(('dp', 'expert')), may hold values from -8 to 8
- expert_outputs: bfloat16 [98304, 3584], P(('dp', 'expert')), may hold values from -6 to 6
- output_grad: bfloat16 [131072, 3584], P(('dp', 'expert')), may hold values from -0.09375 to 0.09375
Outputs:
- expert_inputs: bfloat16 [98304, 3584], P(('dp', 'expert'))
- slot_expert: int32 [98304], P(('dp', 'expert'))
- gate_grads: float32 [131072], P(('dp', 'expert'))
- router_grad: float32 [3584, 256], P('dp', 'expert')
Inputs may be any that keep to these rules, and one draw needn't show every extreme that they name: `route_ids`: each row names 8 different experts; expert e is owned by index e // 16 of the expert axis. Only the first expert of a row is dispatched here; on every device some owner is named first by 6 or more of its tokens. `route_slots`: among one device's 128 tokens whose first expert lies on one owner, in token order, the slots are 0, 1, 2 and so on; pairs with slot 6 or more are dropped.
All inputs are finite; a program needn't handle non-finite values.
Results may differ from a plain program's by a relative error of at most 0.0049.
Values may be sent and summed in bfloat16 or wider, within the bound.
No kernel may reach another device: no remote copies, remote signals or barrier semaphores. Data moves between devices by JAX's collectives and lax.ppermute only.
A program may use at most 128 MiB of HBM per device.

v0:
```python
import jax
import jax.numpy as jnp
from jax import lax
from jax.sharding import PartitionSpec as P

TOPK = 8
EXP_DEV = 16


routed_scale = 2.5


def dequantize(values, scales):
    widened = jnp.repeat(scales.astype(jnp.float32), 128, axis=-1)
    return (values.astype(jnp.float32) * widened).astype(jnp.bfloat16)


def padded_rows(values):
    return jnp.concatenate([values, jnp.zeros((1,) + values.shape[1:], values.dtype)], axis=0)


def shards(
    token_values, block_scales, route_ids, route_slots, router_logits, expert_outputs, output_grad
):
    peer_count = lax.axis_size("expert")
    feature_count = token_values.shape[1]
    slot_cap = expert_outputs.shape[0] // peer_count
    overflow = peer_count * slot_cap
    lead_ids = route_ids[:, 0]
    inside = route_slots < slot_cap
    slot_pos = jnp.where(inside, lead_ids // EXP_DEV * slot_cap + route_slots, overflow)
    dequant = dequantize(token_values, block_scales)
    send_values = (
        jnp.zeros((overflow, feature_count), jnp.bfloat16)
        .at[slot_pos]
        .set(token_values, mode="drop")
    )
    send_scales = (
        jnp.zeros((overflow, block_scales.shape[1]), jnp.bfloat16)
        .at[slot_pos]
        .set(block_scales, mode="drop")
    )
    send_expert = (
        jnp.full((overflow,), -1, jnp.int32).at[slot_pos].set(lead_ids % EXP_DEV, mode="drop")
    )
    got_values, got_scales, got_expert = (
        lax.all_to_all(
            send_values.reshape(peer_count, slot_cap, feature_count),
            "expert",
            split_axis=0,
            concat_axis=0,
            tiled=True,
        ),
        lax.all_to_all(
            send_scales.reshape(peer_count, slot_cap, -1),
            "expert",
            split_axis=0,
            concat_axis=0,
            tiled=True,
        ),
        lax.all_to_all(
            send_expert.reshape(peer_count, slot_cap),
            "expert",
            split_axis=0,
            concat_axis=0,
            tiled=True,
        ),
    )
    expert_inputs = dequantize(got_values, got_scales).reshape(overflow, feature_count)
    slot_expert = got_expert.reshape(-1)
    routed_back = lax.all_to_all(
        expert_outputs.reshape(peer_count, slot_cap, feature_count),
        "expert",
        split_axis=0,
        concat_axis=0,
        tiled=True,
    )
    fetched = padded_rows(routed_back.reshape(overflow, feature_count))[slot_pos]
    gate_grads = jnp.sum(output_grad.astype(jnp.float32) * fetched.astype(jnp.float32), axis=1)
    chosen = jnp.take_along_axis(router_logits, route_ids, axis=1)
    affinity = jax.nn.sigmoid(chosen)
    affinity_sum = jnp.sum(affinity, axis=1, keepdims=True)
    lead_mask = (jnp.arange(TOPK, dtype=jnp.int32) == 0).astype(jnp.float32)[None, :]
    lead_share = affinity[:, 0:1] / affinity_sum
    aff_grad = routed_scale * gate_grads[:, None] * (lead_mask - lead_share) / affinity_sum
    logit_term = aff_grad * affinity * (1.0 - affinity)
    expert_count = router_logits.shape[1]
    matches = route_ids[:, :, None] == jnp.arange(expert_count, dtype=jnp.int32)[None, None, :]
    logit_grad = jnp.sum(jnp.where(matches, logit_term[:, :, None], 0.0), axis=1).astype(
        jnp.bfloat16
    )
    partial_value = lax.psum_scatter(
        lax.dot_general(
            dequant, logit_grad, (((0,), (0,)), ((), ())), preferred_element_type=jnp.float32
        ),
        "dp",
        scatter_dimension=0,
        tiled=True,
    )
    router_grad = lax.psum_scatter(partial_value, "expert", scatter_dimension=1, tiled=True)
    return (expert_inputs, slot_expert, gate_grads, router_grad)


def solution(mesh):
    return jax.shard_map(
        shards,
        mesh=mesh,
        in_specs=(
            P(("dp", "expert"), None),
            P(("dp", "expert"), None),
            P(("dp", "expert"), None),
            P(("dp", "expert")),
            P(("dp", "expert"), None),
            P(("dp", "expert"), None),
            P(("dp", "expert"), None),
        ),
        out_specs=(
            P(("dp", "expert"), None),
            P(("dp", "expert")),
            P(("dp", "expert")),
            P("dp", "expert"),
        ),
        check_vma=False,
    )
```

profile of v0, /device:TPU:14, one launch (start us, length us, event | category | flops | bytes accessed | tf_op | source)
XLA Modules:
  0.0 304.3 jit_solution(5740814472854323738)
XLA Ops:
  7.2 2.2 reshape.100
  9.4 17.9 %all-to-all-start.3 = ((bf16[16,6,3584]{2,1,0:T(8,128)(2,1)}), bf16[16,6,3584]{2,1,0:T(8,128)(2,1)S(1)}, u32[]{:S(2)}, u32[]{:S(2)}) async-start(bf16[16,6,3584]{2,1,0:T(8,128)(2,1)} %reshape.100), calls=%async_computation.3 | async-start | bytes 1835008 | tf_op jit(solution)/shard_map/all_to_all | solution.py:71
  27.7 8.6 %gather_fusion.1 = f32[1024]{0:T(1024)S(1)} fusion(f32[128,256]{1,0:T(8,128)S(1)} %copy-done, s32[1024]{0:T(1024)S(1)} %reshape.112), kind=kCustom, calls=%fused_computation.1 | custom fusion | bytes 16384 | tf_op jit(solution)/shard_map/jit(take_along_axis)/gather | solution.py:80
  36.5 0.6 copy.79
  37.1 0.2 fusion
  37.4 14.6 %all-to-all-done.3 = bf16[16,6,3584]{2,1,0:T(8,128)(2,1)S(1)} async-done(((bf16[16,6,3584]{2,1,0:T(8,128)(2,1)}), bf16[16,6,3584]{2,1,0:T(8,128)(2,1)S(1)}, u32[]{:S(2)}, u32[]{:S(2)}) %all-to-all-start.3) | async-done | bytes 688160 | tf_op jit(solution)/shard_map/all_to_all | solution.py:71
  52.0 0.2 reshape.101
  52.3 1.1 gather_fusion
  53.4 1.5 multiply_reduce_fusion
  55.1 0.4 select_reduce_fusion
  55.5 2.4 fusion.12
  58.0 1.0 scatter_custom_fusion.2
  59.0 0.7 all_to_all.17
  59.7 4.0 %all-to-all-start.2 = ((s32[16,1,6]{2,1,0:T(1,128)}), s32[16,1,6]{2,1,0:T(1,128)S(1)}, u32[]{:S(2)}, u32[]{:S(2)}) async-start(s32[16,1,6]{2,1,0:T(1,128)} %bitcast.1), calls=%async_computation.2 | async-start | bytes 16384 | tf_op jit(solution)/shard_map/all_to_all | solution.py:61
  63.8 0.9 scatter_custom_fusion.1
  64.7 0.6 reshape.96
  65.3 6.8 %all-to-all-done.2 = s32[16,1,6]{2,1,0:T(1,128)S(1)} async-done(((s32[16,1,6]{2,1,0:T(1,128)}), s32[16,1,6]{2,1,0:T(1,128)S(1)}, u32[]{:S(2)}, u32[]{:S(2)}) %all-to-all-start.2) | async-done | bytes 416 | tf_op jit(solution)/shard_map/all_to_all | solution.py:61
  72.1 3.5 %all-to-all-start.1 = ((bf16[16,6,28]{2,1,0:T(8,128)(2,1)}), bf16[16,6,28]{2,1,0:T(8,128)(2,1)S(1)}, u32[]{:S(2)}, u32[]{:S(2)}) async-start(bf16[16,6,28]{2,1,0:T(8,128)(2,1)} %reshape.96), calls=%async_computation.1 | async-start | bytes 65536 | tf_op jit(solution)/shard_map/all_to_all | solution.py:54
  75.6 2.7 scatter_custom_fusion
  78.3 1.2 reshape.95
  79.4 4.7 %all-to-all-done.1 = bf16[16,6,28]{2,1,0:T(8,128)(2,1)S(1)} async-done(((bf16[16,6,28]{2,1,0:T(8,128)(2,1)}), bf16[16,6,28]{2,1,0:T(8,128)(2,1)S(1)}, u32[]{:S(2)}, u32[]{:S(2)}) %all-to-all-start.1) | async-done | bytes 5408 | tf_op jit(solution)/shard_map/all_to_all | solution.py:54
  84.2 4.3 %all-to-all-start = ((bf16[16,6,3584]{2,1,0:T(8,128)(2,1)}), bf16[16,6,3584]{2,1,0:T(8,128)(2,1)}, u32[]{:S(2)}, u32[]{:S(2)}) async-start(bf16[16,6,3584]{2,1,0:T(8,128)(2,1)} %reshape.95), calls=%async_computation | async-start | bytes 1835008 | tf_op jit(solution)/shard_map/all_to_all | solution.py:47
  88.5 0.5 broadcast.112
  89.0 0.7 reduce.3
  89.7 0.6 reshape.99
  90.3 0.5 broadcast_in_dim.56
  90.8 0.2 reshape.97
  91.0 126.3 %reduce-scatter.5.cloned.1.call-done = f32[56,256]{1,0:T(8,128)} async-done(((f32[3584,256]{1,0:T(8,128)}), f32[56,256]{1,0:T(8,128)}) %reduce-scatter.5.cloned.1.call-update) | async-done | bytes 57360 | tf_op jit(solution)/shard_map/reduce_scatter | solution.py:92
  217.3 1.6 copy.85
  218.9 2.0 fusion.1
  220.9 1.1 reshape.98
  222.0 75.5 %reduce-scatter.7.cloned.1.call-done = f32[16,56]{1,0:T(8,128)} async-done(((f32[256,56]{1,0:T(8,128)}), f32[16,56]{1,0:T(8,128)}) %reduce-scatter.7.cloned.1.call-update) | async-done | bytes 3600
  (36 shorter events, 1.0 us)
Async XLA Ops:
  7.2 20.5 %copy-start = (f32[128,256]{1,0:T(8,128)S(1)}, f32[128,256]{1,0:T(8,128)}, u32[]{:S(2)}) copy-start(f32[128,256]{1,0:T(8,128)} %param.11) | copy-start | bytes 393220
  7.2 20.2 %copy-start.3 = (bf16[128,28]{0,1:T(8,128)(2,1)S(1)}, bf16[128,28]{0,1:T(8,128)(2,1)}, u32[]{:S(2)}) copy-start(bf16[128,28]{0,1:T(8,128)(2,1)} %param.8) | copy-start | bytes 21508
  7.2 20.2 %copy-start.2 = (s32[128,8]{0,1:T(8,128)S(1)}, s32[128,8]{0,1:T(8,128)}, u32[]{:S(2)}) copy-start(s32[128,8]{0,1:T(8,128)} %param.9) | copy-start | bytes 12292
  9.4 42.6 %all-to-all-start.3 = ((bf16[16,6,3584]{2,1,0:T(8,128)(2,1)}), bf16[16,6,3584]{2,1,0:T(8,128)(2,1)S(1)}, u32[]{:S(2)}, u32[]{:S(2)}) async-start(bf16[16,6,3584]{2,1,0:T(8,128)(2,1)} %reshape.100), calls=%async_computation.3 | async-start | bytes 1835008 | tf_op jit(solution)/shard_map/all_to_all | solution.py:71
  27.3 190.0 %reduce-scatter.5.cloned.1.call-start = ((), (), s32[]{:S(2)}) async-start(), calls=%async_computation.6 | async-start | bytes 3727360 | tf_op jit(solution)/shard_map/reduce_scatter | solution.py:92
  27.7 8.7 %copy-start.1 = (bf16[128,3584]{1,0:T(8,128)(2,1)S(1)}, bf16[128,3584]{1,0:T(8,128)(2,1)}, u32[]{:S(2)}) copy-start(bf16[128,3584]{1,0:T(8,128)(2,1)} %param.7) | copy-start | bytes 2752516
  36.5 0.8 copy-start.4
  54.9 3.0 %copy-start.5 = (f32[128]{0:T(128)}, f32[128]{0:T(128)S(1)}, u32[]{:S(2)}) copy-start(f32[128]{0:T(128)S(1)} %multiply_reduce_fusion) | copy-start | bytes 1540
  59.7 12.4 %all-to-all-start.2 = ((s32[16,1,6]{2,1,0:T(1,128)}), s32[16,1,6]{2,1,0:T(1,128)S(1)}, u32[]{:S(2)}, u32[]{:S(2)}) async-start(s32[16,1,6]{2,1,0:T(1,128)} %bitcast.1), calls=%async_computation.2 | async-start | bytes 16384 | tf_op jit(solution)/shard_map/all_to_all | solution.py:61
  72.1 12.1 %all-to-all-start.1 = ((bf16[16,6,28]{2,1,0:T(8,128)(2,1)}), bf16[16,6,28]{2,1,0:T(8,128)(2,1)S(1)}, u32[]{:S(2)}, u32[]{:S(2)}) async-start(bf16[16,6,28]{2,1,0:T(8,128)(2,1)} %reshape.96), calls=%async_computation.1 | async-start | bytes 65536 | tf_op jit(solution)/shard_map/all_to_all | solution.py:54
  84.2 134.7 %all-to-all-start = ((bf16[16,6,3584]{2,1,0:T(8,128)(2,1)}), bf16[16,6,3584]{2,1,0:T(8,128)(2,1)}, u32[]{:S(2)}, u32[]{:S(2)}) async-start(bf16[16,6,3584]{2,1,0:T(8,128)(2,1)} %reshape.95), calls=%async_computation | async-start | bytes 1835008 | tf_op jit(solution)/shard_map/all_to_all | solution.py:47
  88.5 209.0 %reduce-scatter.7.cloned.1.call-start = ((), (), s32[]{:S(2)}) async-start(), calls=%async_computation.7 | async-start | bytes 139264
Sparse Core Ops, SparseCore 0:
  58.1 159.1 reduce-scatter.4
  221.6 75.8 reduce-scatter.6
where the time goes:
time: 305 us; the launch traced here: 304 us
  waiting for transfers between devices  228 us (75%)
  starting transfers between devices  29.8 us (10%)
  local copies, waits for them, and re-layouts  24.9 us (8%)
  between operations  14.3 us (5%)
  other arithmetic  4.94 us (2%)
    reduce_scatter x1, waiting for transfers between devices, shards(): lax.psum_scatter(lax.dot_general(dequant, logit_grad, (((0,), (0,)), ((),...  126 us
    unnamed x3, waiting for transfers between devices  75.6 us
    all_to_all x1, starting transfers between devices, shards(): lax.all_to_all(expert_outputs.reshape(peer_count, slot_cap, feature_count...  17.9 us
    all_to_all x1, waiting for transfers between devices, shards(): lax.all_to_all(expert_outputs.reshape(peer_count, slot_cap, feature_count...  14.6 us
    gather x5, local copies, waits for them, and re-layouts, shards(): chosen = jnp.take_along_axis(router_logits, route_ids, axis=1)  8.91 us
    all_to_all x1, waiting for transfers between devices, shards(): lax.all_to_all(send_expert.reshape(peer_count, slot_cap), 'expert', split...  6.76 us
  transfers between devices with their start and end apart: 6, of which 5 were waited for; matrix products, arithmetic and copies ran while one was open for 8% of the time, Pallas kernels for 0%

commit v1 on v0

v1 whole, which is shorter than its diff:
```python
import jax
import jax.numpy as jnp
import numpy as np
from jax import lax
from jax.experimental import pallas as pl
from jax.experimental.pallas import tpu as pltpu
from jax.sharding import Mesh, PartitionSpec as P

D = 3584
TOPK = 8
EXP_DEV = 16
TOK = 128
EXPERTS = 256
BLOCKS = 28
CAP = 6
N_EXPERT = 16
SLOTS = N_EXPERT * CAP
FEAT = 56
CHUNKS = 4
WIDE = D // CHUNKS
PACKED = SLOTS * CHUNKS
META = 16
ROWS = SLOTS + META
PEERS = 16
SCALE = 2.5

ALL = ("yh", "x", "core", "z", "yl")
OWNERS = ("z", "yl")
NEAR = ("x", "core")
FAR = ("yh", "z", "yl")

f32 = jnp.float32
bf16 = jnp.bfloat16


def pack_matrix():
    rows = np.arange(PACKED)
    owner, rest = rows // (CHUNKS * CAP), rows % (CHUNKS * CAP)
    chunk, slot = rest // CAP, rest % CAP
    m = np.zeros((PACKED, PACKED), np.float32)
    m[rows, chunk * SLOTS + owner * CAP + slot] = 1
    return m


def stacked(v):
    return jnp.concatenate([v[:, c * WIDE : (c + 1) * WIDE] for c in range(CHUNKS)], axis=0)


def dot(a, b, **kw):
    return jnp.dot(a, b, preferred_element_type=f32, **kw)


def slot_matrix(lead, slots):
    pos = jnp.where(slots < CAP, (lead >> 4) * CAP + slots, 1000)
    rows = lax.broadcasted_iota(jnp.int32, (TOK, TOK), 0)
    return jnp.where(rows == pos, 1.0, 0.0)


def outgoing(idt_ref, slots_ref, tv_ref, bs_ref, eo_ref, pack_ref, out_ref, deq_ref):
    pick = slot_matrix(idt_ref[0:1, :], slots_ref[...]).astype(bf16)[:SLOTS]
    pack = pack_ref[...]
    out_ref[:, :WIDE] = dot(pack, stacked(eo_ref[...])).astype(bf16)
    scales = dot(pick, bs_ref[...]).astype(bf16)
    block = lax.broadcasted_iota(jnp.int32, (BLOCKS, D), 0)
    lane = lax.broadcasted_iota(jnp.int32, (BLOCKS, D), 1)
    spread = jnp.where((lane >> 7) == block, 1.0, 0.0).astype(bf16)
    deq = (dot(pick, tv_ref[...]) * dot(scales, spread)).astype(bf16)
    deq_ref[...] = deq
    out_ref[:, WIDE:] = dot(pack, stacked(deq)).astype(bf16)


def prepare(idt_ref, slots_ref, ids_ref, logits_ref, og_ref, deq_ref, pack_ref, og_out, near_out):
    pick = slot_matrix(idt_ref[0:1, :], slots_ref[...]).astype(bf16)
    og = dot(pick[:SLOTS], og_ref[...]).astype(bf16)
    og_out[...] = dot(pack_ref[...], stacked(og)).astype(bf16)
    logits = logits_ref[...]
    ids = ids_ref[...]
    wide_lane = lax.broadcasted_iota(jnp.int32, (TOK, EXPERTS), 1)
    lane = lax.broadcasted_iota(jnp.int32, (TOK, TOK), 1)
    chosen = jnp.zeros((TOK, TOK), f32)
    idf = jnp.zeros((TOK, TOK), f32)
    for k in range(TOPK):
        idk = ids[:, k : k + 1]
        one = jnp.sum(jnp.where(wide_lane == idk, logits, 0.0), axis=1, keepdims=True)
        chosen = jnp.where(lane == k, one, chosen)
        idf = jnp.where(lane == k, idk.astype(f32), idf)
    a = 1.0 / (1.0 + jnp.exp(-chosen))
    total = jnp.sum(jnp.where(lane < TOPK, a, 0.0), axis=1, keepdims=True)
    lead = jnp.where(lane == 0, 1.0, 0.0)
    coef = SCALE * (lead - a[:, 0:1] / total) / total * a * (1.0 - a)
    coef = jnp.where(lane < TOPK, coef, 0.0)
    high = coef.astype(bf16).astype(f32)
    low = coef - high
    meta = idf + pltpu.roll(high, TOPK, 1) + pltpu.roll(low, 2 * TOPK, 1)
    meta = jnp.transpose(dot(pick, meta.astype(bf16)))
    top = jnp.concatenate([meta[0:8], meta[8:16]], axis=1)
    bottom = jnp.concatenate([meta[16:24], jnp.zeros((8, TOK), f32)], axis=1)
    block = jnp.concatenate([top, bottom], axis=0).astype(bf16)
    deq = deq_ref[...]
    gap = jnp.zeros((SLOTS, 64 - FEAT), bf16)
    for k in range(PEERS):
        parts = []
        for q in range(CHUNKS):
            at = q * WIDE + k * FEAT
            parts += [deq[:, at : at + FEAT], gap]
        near_out[k, :SLOTS, :] = jnp.concatenate(parts, axis=1)
        near_out[k, SLOTS:, :] = block


def gate(og_ref, got_ref, pack_ref, idt_ref, slots_ref, gate_ref, send_ref):
    prod = og_ref[...].astype(f32) * got_ref[:, :WIDE].astype(f32)
    part = prod[:, :TOK]
    for b in range(1, WIDE // TOK):
        part = part + prod[:, b * TOK : (b + 1) * TOK]
    pack = pack_ref[...].astype(f32)
    fold = pack[:, :SLOTS]
    for c in range(1, CHUNKS):
        fold = fold + pack[:, c * SLOTS : (c + 1) * SLOTS]
    fold = jnp.concatenate([fold, jnp.zeros((PACKED, TOK - SLOTS), f32)], axis=1)
    by_slot = lax.dot_general(
        part, fold, (((0,), (0,)), ((), ())), preferred_element_type=f32, precision=lax.Precision.HIGHEST
    )
    row = jnp.sum(by_slot, axis=0, keepdims=True)
    row = jnp.broadcast_to(row, (8, TOK))
    pick = slot_matrix(idt_ref[0:1, :], slots_ref[...])
    gate_ref[...] = dot(row, pick, precision=lax.Precision.HIGHEST)[0:1]
    send_ref[...] = jnp.broadcast_to(row[None], (PEERS, 8, TOK))


def unpack(got_ref, pack_ref, out_ref):
    got = got_ref[:, WIDE:]
    for c in range(CHUNKS):
        pick = pack_ref[:, c * SLOTS : (c + 1) * SLOTS]
        out_ref[:, c * WIDE : (c + 1) * WIDE] = lax.dot_general(
            pick, got, (((0,), (0,)), ((), ())), preferred_element_type=f32
        ).astype(bf16)


def expand(near_ref, out_ref):
    rows = lax.broadcasted_iota(jnp.int32, (EXPERTS, TOK), 0).astype(f32)
    for s in range(PEERS):
        meta = near_ref[s, SLOTS:, :].astype(f32)
        acc = jnp.zeros((EXPERTS, TOK), f32)
        for k in range(TOPK):
            coef = meta[k : k + 1, TOK:] + meta[8 + k : 9 + k, :TOK]
            acc = acc + jnp.where(rows == meta[k : k + 1, :TOK], coef, 0.0)
        out_ref[s] = acc


def contract(place_ref, near_ref, terms_ref, gg_ref, idt_ref, slots_ref, out_ref, acc_ref):
    yh, mine = place_ref[0], place_ref[1]
    for s in range(PEERS):
        left = (terms_ref[s] * gg_ref[s, 0:1, :]).astype(bf16)[:, :ROWS]
        part = dot(left, near_ref[s])
        if s == 0:
            acc_ref[...] = part
        else:
            acc_ref[...] += part
    lane = lax.broadcasted_iota(jnp.int32, (8, TOK), 1)
    row = lax.broadcasted_iota(jnp.int32, (8, TOK), 0)
    lead = idt_ref[0:1, :]
    pos = jnp.where(slots_ref[...] < CAP, (lead >> 4) * 8 + slots_ref[...], 1000)
    number = jnp.broadcast_to(((lead & 15) + 1).astype(f32), (8, TOK)).astype(bf16)
    srow = lax.broadcasted_iota(jnp.int32, (TOK, TOK), 0)
    place = jnp.where(srow == pos, 1.0, 0.0)
    named = jnp.sum(place * jnp.broadcast_to(((lead & 15) + 1).astype(f32), (TOK, TOK)), axis=1, keepdims=True)
    own_lane = jnp.where(mine < 8, FEAT + mine, 64 + FEAT + mine - 8)
    left_half = lane < 64
    for j in range(PEERS):
        tag = jnp.where(lane == own_lane, named[8 * j : 8 * j + 8], 0.0)
        for h in range(2):
            lo = acc_ref[16 * j : 16 * j + 8, TOK * h : TOK * (h + 1)]
            hi = acc_ref[16 * j + 8 : 16 * j + 16, TOK * h : TOK * (h + 1)]
            first = jnp.where(left_half, lo, pltpu.roll(hi, 64, 1))
            second = jnp.where(left_half, pltpu.roll(lo, 64, 1), hi)
            out_ref[(2 * h) * PEERS + j] = first + jnp.where(yh == 2 * h, tag, 0.0)
            out_ref[(2 * h + 1) * PEERS + j] = second + jnp.where(yh == 2 * h + 1, tag, 0.0)


def finish(far_ref, grad_ref, expert_ref):
    total = jnp.sum(far_ref[...], axis=0)
    grad_ref[0:8, :] = total[:, :FEAT]
    grad_ref[8:16, :] = total[:, 64 : 64 + FEAT]
    lane = lax.broadcasted_iota(jnp.int32, (TOK, TOK), 0)
    slot = lax.broadcasted_iota(jnp.int32, (TOK, TOK), 1)
    source = jnp.where(lane < 64, lane - FEAT, lane - 64 - FEAT + 8)
    tagged = ((lane >= FEAT) & (lane < 64)) | (lane >= 64 + FEAT)
    first = source * CAP
    hit = tagged & (slot >= first) & (slot < first + CAP)
    spread = dot(jnp.where(lax.broadcasted_iota(jnp.int32, (8, TOK), 1) % 64 >= FEAT, total, 0.0), jnp.where(hit, 1.0, 0.0), precision=lax.Precision.HIGHEST)
    row = lax.broadcasted_iota(jnp.int32, (8, TOK), 0)
    col = lax.broadcasted_iota(jnp.int32, (8, TOK), 1)
    value = jnp.sum(jnp.where(col % CAP == row, spread, 0.0), axis=0, keepdims=True)
    expert_ref[...] = (value[:, :SLOTS] + 0.5).astype(jnp.int32) - 1


def call(body, outs, args, flops=0, moved=0, scratch=(), scalars=0):
    specs = [pl.BlockSpec(memory_space=pltpu.SMEM)] * scalars
    specs += [pl.BlockSpec(memory_space=pltpu.VMEM)] * (len(args) - scalars)
    return pl.pallas_call(
        body,
        out_shape=[jax.ShapeDtypeStruct(s, t) for s, t in outs],
        in_specs=specs,
        out_specs=[pl.BlockSpec(memory_space=pltpu.VMEM)] * len(outs),
        scratch_shapes=list(scratch),
        compiler_params=pltpu.CompilerParams(vmem_limit_bytes=40 * 2**20),
        cost_estimate=pl.CostEstimate(flops=flops, bytes_accessed=moved, transcendentals=0),
        name=body.__name__,
    )(*args)


def swap(v, axes):
    return lax.all_to_all(v, axes, split_axis=0, concat_axis=0, tiled=True)


def shards(token_values, block_scales, route_ids, route_slots, router_logits, expert_outputs, output_grad):
    pack = jnp.asarray(pack_matrix(), bf16)
    idt = route_ids.T
    slots = route_slots.reshape(1, TOK)
    place = jnp.stack([lax.axis_index("yh"), lax.axis_index(OWNERS)]).astype(jnp.int32)
    out, deq = call(
        outgoing,
        [((PACKED, 2 * WIDE), bf16), ((SLOTS, D), bf16)],
        (idt, slots, token_values, block_scales, expert_outputs, pack),
    )
    got = swap(out, OWNERS)
    og, near = call(
        prepare,
        [((PACKED, WIDE), bf16), ((PEERS, ROWS, 256), bf16)],
        (idt, slots, route_ids, router_logits, output_grad, deq, pack),
    )
    near = swap(near, NEAR)
    (terms,) = call(expand, [((PEERS, EXPERTS, TOK), f32)], (near,))
    gates, send = call(
        gate, [((1, TOK), f32), ((PEERS, 8, TOK), f32)], (og, got, pack, idt, slots)
    )
    gg = swap(send, NEAR)
    (expert_inputs,) = call(unpack, [((SLOTS, D), bf16)], (got, pack))
    (far,) = call(
        contract,
        [((CHUNKS * PEERS, 8, TOK), f32)],
        (place, near, terms, gg, idt, slots),
        scratch=[pltpu.VMEM((EXPERTS, 256), f32)],
        scalars=1,
    )
    far = swap(far, FAR)
    grad, named = call(finish, [((EXP_DEV, FEAT), f32), ((1, SLOTS), jnp.int32)], (far,))
    return expert_inputs, named.reshape(SLOTS), gates.reshape(TOK), grad.T


def solution(mesh):
    fine = Mesh(mesh.devices.reshape(4, 8, 2, 8, 2), ALL)
    rows = P(ALL, None)
    return jax.shard_map(
        shards,
        mesh=fine,
        in_specs=(rows, rows, rows, P(ALL), rows, rows, rows),
        out_specs=(rows, P(ALL), P(ALL), P(("yh", "x", "core"), ("z", "yl"))),
        check_vma=False,
    )
```

time: 305 us -> 133 us (0.44)
  the two profiles are of different devices: /device:TPU:14 before, /device:TPU:1 now
where the time goes in v1:
time: 133 us; the launch traced here: 132 us
  waiting for transfers between devices  66.8 us (50%)
  starting transfers between devices  40.7 us (31%)
  local copies, waits for them, and re-layouts  12.4 us (9%)
  Pallas kernels  11 us (8%)
    all_to_all x4, waiting for transfers between devices, swap(): return lax.all_to_all(v, axes, split_axis=0, concat_axis=0, tiled=True)  66.8 us
    all_to_all x4, starting transfers between devices, swap(): return lax.all_to_all(v, axes, split_axis=0, concat_axis=0, tiled=True)  40.7 us
    unnamed x38, local copies, waits for them, and re-layouts  12.4 us
    pallas_call x7, Pallas kernels, call(): pl.pallas_call(body, out_shape=[jax.ShapeDtypeStruct(s, t) for s, t in ou...  11 us
  transfers between devices with their start and end apart: 4, of which 4 were waited for; matrix products, arithmetic and copies ran while one was open for 0% of the time, Pallas kernels for 6%

profile of v1, /device:TPU:1, one launch (start us, length us, event | category | flops | bytes accessed | tf_op | source)
XLA Modules:
  0.0 131.8 jit_solution(17410138902662109034)
XLA Ops:
  0.6 0.8 copy.12.bs_ref
  1.5 1.0 copy-done.3
  2.4 1.2 copy-done.9
  3.6 1.1 copy-done.10
  4.7 0.7 copy-done.14
  5.4 0.7 copy-done.16
  6.0 1.4 %outgoing.1 = (bf16[384,1792]{1,0:T(8,128)(2,1)S(1)}, bf16[96,3584]{1,0:T(8,128)(2,1)S(1)}) custom-call(s32[8,128]{1,0:T(8,128)S(1)} %bitcast.12, s32[1,128]{1,0:T(1,128)S(1)} %bitcast.16, bf16[128,3584]{1,0:T(8,128)(2,1)S(1)} %copy-done.9, bf16[128,28]{1,0:T(8,128)(2,1)S(1)} %copy.12.bs_ref, bf16[96,3584]{1,0:T(8,128)(2,1)S(1)} %copy-done.10, ...), custom_call_target="tpu_custom_call" | custom-call | tf_op jit(solution)/shard_map/outgoing/pallas_call | solution.py:200
  7.5 1.1 copy-done.6
  8.6 0.0 copy-start.17
  8.6 18.6 %all-to-all-start = ((bf16[16,24,1792]{2,1,0:T(8,128)(2,1)}), bf16[16,24,1792]{2,1,0:T(8,128)(2,1)S(1)}, u32[]{:S(2)}, u32[]{:S(2)}) async-start(bf16[16,24,1792]{2,1,0:T(8,128)(2,1)} %bitcast.11), calls=%async_computation | async-start | bytes 2752512 | tf_op jit(solution)/shard_map/all_to_all | solution.py:213
  27.2 0.1 copy.13.ids_ref
  27.3 3.1 %prepare.1 = (bf16[384,896]{1,0:T(8,128)(2,1)S(1)}, bf16[16,112,256]{2,1,0:T(8,128)(2,1)}) custom-call(s32[8,128]{1,0:T(8,128)S(1)} %bitcast.13, s32[1,128]{1,0:T(1,128)S(1)} %bitcast.17, s32[128,8]{1,0:T(8,128)S(1)} %copy.13.ids_ref, f32[128,256]{1,0:T(8,128)S(1)} %copy-done.13, bf16[128,3584]{1,0:T(8,128)(2,1)S(1)} %copy-done.8, ...), custom_call_target="tpu_custom_call" | custom-call | tf_op jit(solution)/shard_map/prepare/pallas_call | solution.py:200
  30.4 0.8 copy-done.11
  31.3 28.3 %all-to-all-done = bf16[16,24,1792]{2,1,0:T(8,128)(2,1)S(1)} async-done(((bf16[16,24,1792]{2,1,0:T(8,128)(2,1)}), bf16[16,24,1792]{2,1,0:T(8,128)(2,1)S(1)}, u32[]{:S(2)}, u32[]{:S(2)}) %all-to-all-start) | async-done | bytes 1376288 | tf_op jit(solution)/shard_map/all_to_all | solution.py:213
  59.6 10.3 %all-to-all-start.1 = ((bf16[16,112,256]{2,1,0:T(8,128)(2,1)}), bf16[16,112,256]{2,1,0:T(8,128)(2,1)S(1)}, u32[]{:S(2)}, u32[]{:S(2)}) async-start(bf16[16,112,256]{2,1,0:T(8,128)(2,1)} %get-tuple-element.14), calls=%async_computation.1 | async-start | bytes 1835008 | tf_op jit(solution)/shard_map/all_to_all | solution.py:213
  70.0 1.4 %gate.1 = (f32[1,128]{1,0:T(1,128)}, f32[16,8,128]{2,1,0:T(8,128)}) custom-call(bf16[384,896]{1,0:T(8,128)(2,1)S(1)} %copy-done.12, bf16[384,1792]{1,0:T(8,128)(2,1)S(1)} %bitcast.9, bf16[384,384]{1,0:T(8,128)(2,1)S(1)} %copy-done.4, s32[8,128]{1,0:T(8,128)S(1)} %bitcast.14, s32[1,128]{1,0:T(1,128)S(1)} %bitcast.18), custom_call_target="tpu_custom_call" | custom-call | tf_op jit(solution)/shard_map/gate/pallas_call | solution.py:200
  71.3 23.9 %all-to-all-done.1.near_ref = bf16[16,112,256]{2,1,0:T(8,128)(2,1)S(1)} async-done(((bf16[16,112,256]{2,1,0:T(8,128)(2,1)}), bf16[16,112,256]{2,1,0:T(8,128)(2,1)S(1)}, u32[]{:S(2)}, u32[]{:S(2)}) %all-to-all-start.1) | async-done | bytes 917536 | tf_op jit(solution)/shard_map/all_to_all | solution.py:213
  95.3 0.9 copy-done
  96.2 3.4 %all-to-all-start.2 = ((f32[16,8,128]{2,1,0:T(8,128)}), f32[16,8,128]{2,1,0:T(8,128)S(1)}, u32[]{:S(2)}, u32[]{:S(2)}) async-start(f32[16,8,128]{2,1,0:T(8,128)} %get-tuple-element.16), calls=%async_computation.2 | async-start | bytes 131072 | tf_op jit(solution)/shard_map/all_to_all | solution.py:213
  99.6 0.1 pad_add_fusion.place_ref
  99.7 1.2 copy-done.1
  100.9 1.6 %expand.1.terms_ref = f32[16,256,128]{2,1,0:T(8,128)S(1)} custom-call(bf16[16,112,256]{2,1,0:T(8,128)(2,1)S(1)} %copy-done.1), custom_call_target="tpu_custom_call" | custom-call | tf_op jit(solution)/shard_map/expand/pallas_call | solution.py:200
  102.5 4.9 %all-to-all-done.2.gg_ref = f32[16,8,128]{2,1,0:T(8,128)S(1)} async-done(((f32[16,8,128]{2,1,0:T(8,128)}), f32[16,8,128]{2,1,0:T(8,128)S(1)}, u32[]{:S(2)}, u32[]{:S(2)}) %all-to-all-start.2) | async-done | bytes 65568 | tf_op jit(solution)/shard_map/all_to_all | solution.py:213
  107.4 1.2 copy-done.2
  108.5 1.3 contract.1
  109.9 0.7 copy-done.7
  110.6 8.4 %all-to-all-start.3 = ((f32[64,8,128]{2,1,0:T(8,128)}), f32[64,8,128]{2,1,0:T(8,128)S(1)}, u32[]{:S(2)}, u32[]{:S(2)}) async-start(f32[64,8,128]{2,1,0:T(8,128)} %copy-done.7), calls=%async_computation.3 | async-start | bytes 524288 | tf_op jit(solution)/shard_map/all_to_all | solution.py:213
  118.9 0.0 copy-start.5
  118.9 1.0 copy-done.5
  119.9 1.5 %unpack.1 = bf16[96,3584]{1,0:T(8,128)(2,1)} custom-call(bf16[384,1792]{1,0:T(8,128)(2,1)S(1)} %bitcast.10, bf16[384,384]{1,0:T(8,128)(2,1)S(1)} %copy-done.5), custom_call_target="tpu_custom_call" | custom-call | tf_op jit(solution)/shard_map/unpack/pallas_call | solution.py:200
  121.4 9.6 %all-to-all-done.3.far_ref = f32[64,8,128]{2,1,0:T(8,128)S(1)} async-done(((f32[64,8,128]{2,1,0:T(8,128)}), f32[64,8,128]{2,1,0:T(8,128)S(1)}, u32[]{:S(2)}, u32[]{:S(2)}) %all-to-all-start.3) | async-done | bytes 262176 | tf_op jit(solution)/shard_map/all_to_all | solution.py:213
  131.0 0.7 finish.1
  (22 shorter events, 0.0 us)
Async XLA Ops:
  1.5 1.0 copy-start.3
  2.4 1.2 copy-start.9
  3.6 1.1 copy-start.10
  4.7 0.7 copy-start.14
  5.4 0.7 copy-start.16
  7.4 1.1 copy-start.6
  8.5 18.6 %copy-start.15 = (s32[128,8]{0,1:T(8,128)S(1)}, s32[128,8]{0,1:T(8,128)}, u32[]{:S(2)}) copy-start(s32[128,8]{0,1:T(8,128)} %param.10) | copy-start | bytes 12292
  8.6 18.7 %copy-start.4 = (bf16[384,384]{1,0:T(8,128)(2,1)S(1)}, bf16[384,384]{1,0:T(8,128)(2,1)}, u32[]{:S(2)}) copy-start(bf16[384,384]{1,0:T(8,128)(2,1)} %constant.18.clone.pack_ref) | copy-start | bytes 884740
  8.6 18.7 %copy-start.8 = (bf16[128,3584]{1,0:T(8,128)(2,1)S(1)}, bf16[128,3584]{1,0:T(8,128)(2,1)}, u32[]{:S(2)}) copy-start(bf16[128,3584]{1,0:T(8,128)(2,1)} %og_ref.1) | copy-start | bytes 2752516
  8.6 18.8 %copy-start.13 = (f32[128,256]{1,0:T(8,128)S(1)}, f32[128,256]{1,0:T(8,128)}, u32[]{:S(2)}) copy-start(f32[128,256]{1,0:T(8,128)} %logits_ref.1) | copy-start | bytes 393220
  8.6 18.8 %copy-start.17 = (s32[128]{0:T(128)S(1)}, s32[128]{0:T(128)}, u32[]{:S(2)}) copy-start(s32[128]{0:T(128)} %param.11) | copy-start | bytes 1540
  8.6 51.1 %all-to-all-start = ((bf16[16,24,1792]{2,1,0:T(8,128)(2,1)}), bf16[16,24,1792]{2,1,0:T(8,128)(2,1)S(1)}, u32[]{:S(2)}, u32[]{:S(2)}) async-start(bf16[16,24,1792]{2,1,0:T(8,128)(2,1)} %bitcast.11), calls=%async_computation | async-start | bytes 2752512 | tf_op jit(solution)/shard_map/all_to_all | solution.py:213
  30.4 0.8 copy-start.11
  59.6 10.3 %copy-start.12 = (bf16[384,896]{1,0:T(8,128)(2,1)S(1)}, bf16[384,896]{1,0:T(8,128)(2,1)}, u32[]{:S(2)}) copy-start(bf16[384,896]{1,0:T(8,128)(2,1)} %copy-done.11) | copy-start | bytes 2064388
  59.6 35.6 %all-to-all-start.1 = ((bf16[16,112,256]{2,1,0:T(8,128)(2,1)}), bf16[16,112,256]{2,1,0:T(8,128)(2,1)S(1)}, u32[]{:S(2)}, u32[]{:S(2)}) async-start(bf16[16,112,256]{2,1,0:T(8,128)(2,1)} %get-tuple-element.14), calls=%async_computation.1 | async-start | bytes 1835008 | tf_op jit(solution)/shard_map/all_to_all | solution.py:213
  95.3 0.9 copy-start
  96.2 11.2 %all-to-all-start.2 = ((f32[16,8,128]{2,1,0:T(8,128)}), f32[16,8,128]{2,1,0:T(8,128)S(1)}, u32[]{:S(2)}, u32[]{:S(2)}) async-start(f32[16,8,128]{2,1,0:T(8,128)} %get-tuple-element.16), calls=%async_computation.2 | async-start | bytes 131072 | tf_op jit(solution)/shard_map/all_to_all | solution.py:213
  99.7 1.2 copy-start.1
  107.4 1.2 copy-start.2
  109.9 0.7 copy-start.7
  110.6 20.5 %all-to-all-start.3 = ((f32[64,8,128]{2,1,0:T(8,128)}), f32[64,8,128]{2,1,0:T(8,128)S(1)}, u32[]{:S(2)}, u32[]{:S(2)}) async-start(f32[64,8,128]{2,1,0:T(8,128)} %copy-done.7), calls=%async_computation.3 | async-start | bytes 524288 | tf_op jit(solution)/shard_map/all_to_all | solution.py:213
  118.9 1.0 copy-start.5

commit v2 on v1

--- a/solution.py
+++ b/solution.py
@@ -22,6 +22,9 @@
 META = 16
 ROWS = SLOTS + META
 PEERS = 16
+RING = 8
+STEPS = (0, 4, 3, 5, 2, 6, 1, 7)
+HELD = 7
 SCALE = 2.5
 
 ALL = ("yh", "x", "core", "z", "yl")
@@ -56,23 +59,52 @@
     return jnp.where(rows == pos, 1.0, 0.0)
 
 
-def outgoing(idt_ref, slots_ref, tv_ref, bs_ref, eo_ref, pack_ref, out_ref, deq_ref):
+def outgoing(idt_hbm, slots_hbm, tv_hbm, bst_hbm, eo_hbm, pack_hbm, out_hbm, deq_hbm,
+             idt_ref, slots_ref, tv_ref, bst_ref, eo_ref, pack_ref, back_ref, rows_ref, deq_ref, sems, out_sems):
+    pairs = [
+        (eo_hbm, eo_ref),
+        (pack_hbm, pack_ref),
+        (idt_hbm, idt_ref),
+        (slots_hbm, slots_ref),
+        (bst_hbm, bst_ref),
+        (tv_hbm, tv_ref),
+    ]
+    copies = [pltpu.make_async_copy(a, b, sems.at[n]) for n, (a, b) in enumerate(pairs)]
+    for c in copies:
+        c.start()
+    copies[0].wait()
+    copies[1].wait()
+    pack = pack_ref[...]
+    back_ref[...] = dot(pack, stacked(eo_ref[...])).astype(bf16)
+    back_out = pltpu.make_async_copy(back_ref, out_hbm.at[:, pl.ds(0, WIDE)], out_sems.at[0])
+    back_out.start()
+    for c in copies[2:]:
+        c.wait()
     pick = slot_matrix(idt_ref[0:1, :], slots_ref[...]).astype(bf16)[:SLOTS]
-    pack = pack_ref[...]
-    out_ref[:, :WIDE] = dot(pack, stacked(eo_ref[...])).astype(bf16)
-    scales = dot(pick, bs_ref[...]).astype(bf16)
+    scales = lax.dot_general(
+        pick, bst_ref[...], (((1,), (1,)), ((), ())), preferred_element_type=f32
+    ).astype(bf16)
     block = lax.broadcasted_iota(jnp.int32, (BLOCKS, D), 0)
     lane = lax.broadcasted_iota(jnp.int32, (BLOCKS, D), 1)
     spread = jnp.where((lane >> 7) == block, 1.0, 0.0).astype(bf16)
     deq = (dot(pick, tv_ref[...]) * dot(scales, spread)).astype(bf16)
     deq_ref[...] = deq
-    out_ref[:, WIDE:] = dot(pack, stacked(deq)).astype(bf16)
-
-
-def prepare(idt_ref, slots_ref, ids_ref, logits_ref, og_ref, deq_ref, pack_ref, og_out, near_out):
+    deq_out = pltpu.make_async_copy(deq_ref, deq_hbm, out_sems.at[2])
+    deq_out.start()
+    rows_ref[...] = dot(pack, stacked(deq)).astype(bf16)
+    rows_out = pltpu.make_async_copy(rows_ref, out_hbm.at[:, pl.ds(WIDE, WIDE)], out_sems.at[1])
+    rows_out.start()
+    deq_out.wait()
+    back_out.wait()
+    rows_out.wait()
+
+
+def prepare(place_ref, idt_ref, slots_ref, ids_ref, logits_ref, og_ref, deq_ref, pack_ref, og_hbm, own_out, other_out, og_out, og_sem):
     pick = slot_matrix(idt_ref[0:1, :], slots_ref[...]).astype(bf16)
     og = dot(pick[:SLOTS], og_ref[...]).astype(bf16)
     og_out[...] = dot(pack_ref[...], stacked(og)).astype(bf16)
+    og_copy = pltpu.make_async_copy(og_out, og_hbm, og_sem)
+    og_copy.start()
     logits = logits_ref[...]
     ids = ids_ref[...]
     wide_lane = lax.broadcasted_iota(jnp.int32, (TOK, EXPERTS), 1)
@@ -98,13 +130,27 @@
     block = jnp.concatenate([top, bottom], axis=0).astype(bf16)
     deq = deq_ref[...]
     gap = jnp.zeros((SLOTS, 64 - FEAT), bf16)
-    for k in range(PEERS):
-        parts = []
-        for q in range(CHUNKS):
-            at = q * WIDE + k * FEAT
-            parts += [deq[:, at : at + FEAT], gap]
-        near_out[k, :SLOTS, :] = jnp.concatenate(parts, axis=1)
-        near_out[k, SLOTS:, :] = block
+    x, core = place_ref[2], place_ref[3]
+    for far_x in range(RING):
+        step = (far_x - x) & (RING - 1)
+        pieces = []
+        for k in (2 * far_x, 2 * far_x + 1):
+            parts = []
+            for q in range(CHUNKS):
+                at = q * WIDE + k * FEAT
+                parts += [deq[:, at : at + FEAT], gap]
+            pieces.append(jnp.concatenate(parts, axis=1))
+        own_out[step, :SLOTS, :] = jnp.where(core == 0, pieces[0], pieces[1])
+        other_out[step, :SLOTS, :] = jnp.where(core == 0, pieces[1], pieces[0])
+        own_out[step, SLOTS:, :] = block
+        other_out[step, SLOTS:, :] = block
+    og_copy.wait()
+
+
+def join(own_ref, other_ref, *outs):
+    for step in range(RING):
+        outs[step][:ROWS, :] = own_ref[step]
+        outs[step][ROWS:, :] = other_ref[step]
 
 
 def gate(og_ref, got_ref, pack_ref, idt_ref, slots_ref, gate_ref, send_ref):
@@ -136,23 +182,24 @@
         ).astype(bf16)
 
 
-def expand(near_ref, out_ref):
+def contract(place_ref, gg_ref, idt_ref, slots_ref, *refs):
+    near_refs = refs[:RING]
+    out_hbm, acc_ref, out_ref, out_sem = refs[RING:]
+    yh, mine, x, core = (place_ref[n] for n in range(4))
     rows = lax.broadcasted_iota(jnp.int32, (EXPERTS, TOK), 0).astype(f32)
-    for s in range(PEERS):
-        meta = near_ref[s, SLOTS:, :].astype(f32)
-        acc = jnp.zeros((EXPERTS, TOK), f32)
-        for k in range(TOPK):
-            coef = meta[k : k + 1, TOK:] + meta[8 + k : 9 + k, :TOK]
-            acc = acc + jnp.where(rows == meta[k : k + 1, :TOK], coef, 0.0)
-        out_ref[s] = acc
-
-
-def contract(place_ref, near_ref, terms_ref, gg_ref, idt_ref, slots_ref, out_ref, acc_ref):
-    yh, mine = place_ref[0], place_ref[1]
-    for s in range(PEERS):
-        left = (terms_ref[s] * gg_ref[s, 0:1, :]).astype(bf16)[:, :ROWS]
-        part = dot(left, near_ref[s])
-        if s == 0:
+    for n, step in enumerate(STEPS):
+        left = []
+        for o in range(2):
+            at = o * ROWS + SLOTS
+            meta = near_refs[n][at : at + META, :].astype(f32)
+            source = ((x - step) & (RING - 1)) * 2 + (core ^ o)
+            term = jnp.zeros((EXPERTS, TOK), f32)
+            for k in range(TOPK):
+                coef = meta[k : k + 1, TOK:] + meta[8 + k : 9 + k, :TOK]
+                term = term + jnp.where(rows == meta[k : k + 1, :TOK], coef * gg_ref[source, 0:1, :], 0.0)
+            left.append(term.astype(bf16)[:, :ROWS])
+        part = dot(jnp.concatenate(left, axis=1), near_refs[n][...])
+        if n == 0:
             acc_ref[...] = part
         else:
             acc_ref[...] += part
@@ -160,7 +207,6 @@
     row = lax.broadcasted_iota(jnp.int32, (8, TOK), 0)
     lead = idt_ref[0:1, :]
     pos = jnp.where(slots_ref[...] < CAP, (lead >> 4) * 8 + slots_ref[...], 1000)
-    number = jnp.broadcast_to(((lead & 15) + 1).astype(f32), (8, TOK)).astype(bf16)
     srow = lax.broadcasted_iota(jnp.int32, (TOK, TOK), 0)
     place = jnp.where(srow == pos, 1.0, 0.0)
     named = jnp.sum(place * jnp.broadcast_to(((lead & 15) + 1).astype(f32), (TOK, TOK)), axis=1, keepdims=True)
@@ -173,12 +219,15 @@
             hi = acc_ref[16 * j + 8 : 16 * j + 16, TOK * h : TOK * (h + 1)]
             first = jnp.where(left_half, lo, pltpu.roll(hi, 64, 1))
             second = jnp.where(left_half, pltpu.roll(lo, 64, 1), hi)
-            out_ref[(2 * h) * PEERS + j] = first + jnp.where(yh == 2 * h, tag, 0.0)
-            out_ref[(2 * h + 1) * PEERS + j] = second + jnp.where(yh == 2 * h + 1, tag, 0.0)
-
+            out_ref[(2 * h) * PEERS + j] = (first + jnp.where(yh == 2 * h, tag, 0.0)).astype(bf16)
+            out_ref[(2 * h + 1) * PEERS + j] = (second + jnp.where(yh == 2 * h + 1, tag, 0.0)).astype(bf16)
+
+    out_copy = pltpu.make_async_copy(out_ref, out_hbm, out_sem)
+    out_copy.start()
+    out_copy.wait()
 
 def finish(far_ref, grad_ref, expert_ref):
-    total = jnp.sum(far_ref[...], axis=0)
+    total = jnp.sum(far_ref[...].astype(f32), axis=0)
     grad_ref[0:8, :] = total[:, :FEAT]
     grad_ref[8:16, :] = total[:, 64 : 64 + FEAT]
     lane = lax.broadcasted_iota(jnp.int32, (TOK, TOK), 0)
@@ -194,17 +243,18 @@
     expert_ref[...] = (value[:, :SLOTS] + 0.5).astype(jnp.int32) - 1
 
 
-def call(body, outs, args, flops=0, moved=0, scratch=(), scalars=0):
+def call(body, outs, args, scratch=(), scalars=0, hbm_in=False, hbm_last=0, hbm_out=(), limit=32):
+    vmem, hbm = pl.BlockSpec(memory_space=pltpu.VMEM), pl.BlockSpec(memory_space=pl.ANY)
     specs = [pl.BlockSpec(memory_space=pltpu.SMEM)] * scalars
-    specs += [pl.BlockSpec(memory_space=pltpu.VMEM)] * (len(args) - scalars)
+    specs += [hbm if hbm_in else vmem] * (len(args) - scalars)
+    specs[len(specs) - hbm_last :] = [hbm] * hbm_last
     return pl.pallas_call(
         body,
         out_shape=[jax.ShapeDtypeStruct(s, t) for s, t in outs],
         in_specs=specs,
-        out_specs=[pl.BlockSpec(memory_space=pltpu.VMEM)] * len(outs),
+        out_specs=[hbm if n in hbm_out else vmem for n in range(len(outs))],
         scratch_shapes=list(scratch),
-        compiler_params=pltpu.CompilerParams(vmem_limit_bytes=40 * 2**20),
-        cost_estimate=pl.CostEstimate(flops=flops, bytes_accessed=moved, transcendentals=0),
+        compiler_params=pltpu.CompilerParams(vmem_limit_bytes=limit * 2**20),
         name=body.__name__,
     )(*args)
 
@@ -217,20 +267,45 @@
     pack = jnp.asarray(pack_matrix(), bf16)
     idt = route_ids.T
     slots = route_slots.reshape(1, TOK)
-    place = jnp.stack([lax.axis_index("yh"), lax.axis_index(OWNERS)]).astype(jnp.int32)
+    place = jnp.stack(
+        [lax.axis_index("yh"), lax.axis_index(OWNERS), lax.axis_index("x"), lax.axis_index("core")]
+    ).astype(jnp.int32)
     out, deq = call(
         outgoing,
         [((PACKED, 2 * WIDE), bf16), ((SLOTS, D), bf16)],
-        (idt, slots, token_values, block_scales, expert_outputs, pack),
+        (idt, slots, token_values, block_scales.T, expert_outputs, pack),
+        scratch=[
+            pltpu.VMEM((TOPK, TOK), jnp.int32),
+            pltpu.VMEM((1, TOK), jnp.int32),
+            pltpu.VMEM((TOK, D), bf16),
+            pltpu.VMEM((BLOCKS, TOK), bf16),
+            pltpu.VMEM((SLOTS, D), bf16),
+            pltpu.VMEM((PACKED, PACKED), bf16),
+            pltpu.VMEM((PACKED, WIDE), bf16),
+            pltpu.VMEM((PACKED, WIDE), bf16),
+            pltpu.VMEM((SLOTS, D), bf16),
+            pltpu.SemaphoreType.DMA((6,)),
+            pltpu.SemaphoreType.DMA((3,)),
+        ],
+        hbm_in=True,
+        hbm_out=(0, 1),
+        limit=58,
     )
     got = swap(out, OWNERS)
-    og, near = call(
+    og, own, other = call(
         prepare,
-        [((PACKED, WIDE), bf16), ((PEERS, ROWS, 256), bf16)],
-        (idt, slots, route_ids, router_logits, output_grad, deq, pack),
-    )
-    near = swap(near, NEAR)
-    (terms,) = call(expand, [((PEERS, EXPERTS, TOK), f32)], (near,))
+        [((PACKED, WIDE), bf16), ((RING, ROWS, 256), bf16), ((RING, ROWS, 256), bf16)],
+        (place, idt, slots, route_ids, router_logits, output_grad, deq, pack),
+        scratch=[pltpu.VMEM((PACKED, WIDE), bf16), pltpu.SemaphoreType.DMA],
+        scalars=1,
+        hbm_out=(0,),
+    )
+    other = lax.ppermute(other, "core", [(0, 1), (1, 0)])
+    joined = call(join, [((2 * ROWS, 256), bf16)] * RING, (own, other))
+    near = [joined[0]]
+    for step in STEPS[1:]:
+        near.append(lax.ppermute(joined[step], "x", [(i, (i + step) % RING) for i in range(RING)]))
+    got, og, *near[:HELD] = lax.optimization_barrier((got, og, *near[:HELD]))
     gates, send = call(
         gate, [((1, TOK), f32), ((PEERS, 8, TOK), f32)], (og, got, pack, idt, slots)
     )
@@ -238,10 +313,16 @@
     (expert_inputs,) = call(unpack, [((SLOTS, D), bf16)], (got, pack))
     (far,) = call(
         contract,
-        [((CHUNKS * PEERS, 8, TOK), f32)],
-        (place, near, terms, gg, idt, slots),
-        scratch=[pltpu.VMEM((EXPERTS, 256), f32)],
+        [((CHUNKS * PEERS, 8, TOK), bf16)],
+        (place, gg, idt, slots, *near),
+        scratch=[
+            pltpu.VMEM((EXPERTS, 256), f32),
+            pltpu.VMEM((CHUNKS * PEERS, 8, TOK), bf16),
+            pltpu.SemaphoreType.DMA,
+        ],
         scalars=1,
+        hbm_out=(0,),
+        limit=32,
     )
     far = swap(far, FAR)
     grad, named = call(finish, [((EXP_DEV, FEAT), f32), ((1, SLOTS), jnp.int32)], (far,))

time: 133 us -> 107 us (0.80)
  waiting for transfers between devices: 66.8 us -> 18.8 us
  starting transfers between devices: 40.7 us -> 70.1 us
  local copies, waits for them, and re-layouts: 12.4 us -> 0.99 us
  Pallas kernels: 11 us -> 14.3 us
    all_to_all x4 -> x3, waiting for transfers between devices: 66.8 us -> 10.5 us  [swap(): return lax.all_to_all(v, axes, split_axis=0, concat_axis=0, tiled=True)]
    ppermute x0 -> x8, starting transfers between devices: none -> 32.6 us  [the longest x7 29.6 us: shards(): lax.ppermute(joined[step], 'x', [(i, (i + step) % RING) for i in range(RI...]
    unnamed x38 -> x17, local copies, waits for them, and re-layouts: 12.4 us -> 0.99 us
    ppermute x0 -> x8, waiting for transfers between devices: none -> 8.32 us  [the longest x7 6.9 us: shards(): lax.ppermute(joined[step], 'x', [(i, (i + step) % RING) for i in range(RI...]
    pallas_call x7, Pallas kernels: 11 us -> 14.3 us  [call(): pl.pallas_call(body, out_shape=[jax.ShapeDtypeStruct(s, t) for s, t in ou...]
    all_to_all x4 -> x3, starting transfers between devices: 40.7 us -> 37.5 us  [swap(): return lax.all_to_all(v, axes, split_axis=0, concat_axis=0, tiled=True)]
  transfers between devices with their start and end apart: 4 -> 11, of which waited for: 4 -> 6; matrix products, arithmetic and copies ran while one was open for 0% -> 0% of each run, Pallas kernels for 6% -> 5%
where the time goes in v2:
time: 107 us; the launch traced here: 105 us
  starting transfers between devices  70.1 us (66%)
  waiting for transfers between devices  18.8 us (18%)
  Pallas kernels  14.3 us (13%)
    all_to_all x3, starting transfers between devices, swap(): return lax.all_to_all(v, axes, split_axis=0, concat_axis=0, tiled=True)  37.5 us
    ppermute x7, starting transfers between devices, shards(): lax.ppermute(joined[step], 'x', [(i, (i + step) % RING) for i in range(RI...  29.6 us
    pallas_call x7, Pallas kernels, call(): pl.pallas_call(body, out_shape=[jax.ShapeDtypeStruct(s, t) for s, t in ou...  14.3 us
    all_to_all x3, waiting for transfers between devices, swap(): return lax.all_to_all(v, axes, split_axis=0, concat_axis=0, tiled=True)  10.5 us
    ppermute x7, waiting for transfers between devices, shards(): lax.ppermute(joined[step], 'x', [(i, (i + step) % RING) for i in range(RI...  6.9 us
    ppermute x1, starting transfers between devices, shards(): other = lax.ppermute(other, 'core', [(0, 1), (1, 0)])  2.99 us
  transfers between devices with their start and end apart: 11, of which 6 were waited for; matrix products, arithmetic and copies ran while one was open for 0% of the time, Pallas kernels for 5%

profile of v2, /device:TPU:1, one launch (start us, length us, event | category | flops | bytes accessed | tf_op | source)
XLA Modules:
  0.0 105.1 jit_solution(6040241716240376442)
XLA Ops:
  0.6 3.7 %outgoing.1 = (bf16[384,1792]{1,0:T(8,128)(2,1)}, bf16[96,3584]{1,0:T(8,128)(2,1)}) custom-call(s32[8,128]{1,0:T(8,128)} %bitcast.14, s32[1,128]{1,0:T(1,128)} %bitcast.18, bf16[128,3584]{1,0:T(8,128)(2,1)} %tv_hbm.1, bf16[28,128]{1,0:T(8,128)(2,1)} %bitcast.23, bf16[96,3584]{1,0:T(8,128)(2,1)} %eo_hbm.1, bf16[384,384]{1,0:T(8,128)(2,1)} %constant.26.clone.pack_hbm.pack_ref), custom_call_target="tpu_custom_call" | custom-call | tf_op jit(solution)/shard_map/outgoing/pallas_call | solution.py:251
  4.4 0.0 copy-start
  4.4 0.0 copy-start.1
  4.4 0.0 copy-start.5
  4.4 0.0 copy-start.7
  4.4 18.6 %all-to-all-start = ((bf16[16,24,1792]{2,1,0:T(8,128)(2,1)}), bf16[16,24,1792]{2,1,0:T(8,128)(2,1)S(1)}, u32[]{:S(2)}, u32[]{:S(2)}) async-start(bf16[16,24,1792]{2,1,0:T(8,128)(2,1)} %bitcast.22), calls=%async_computation | async-start | bytes 2752512 | tf_op jit(solution)/shard_map/all_to_all | solution.py:263
  23.1 0.1 copy.12.ids_ref
  23.2 0.1 pad_add_fusion.place_ref
  23.3 3.8 %prepare.1 = (bf16[384,896]{1,0:T(8,128)(2,1)S(1)}, bf16[8,112,256]{2,1,0:T(8,128)(2,1)S(1)}, bf16[8,112,256]{2,1,0:T(8,128)(2,1)S(1)}) custom-call(s32[4]{0:T(128)S(1)} %pad_add_fusion.place_ref, s32[8,128]{1,0:T(8,128)S(1)} %bitcast.15, s32[1,128]{1,0:T(1,128)S(1)} %bitcast.19, s32[128,8]{1,0:T(8,128)S(1)} %copy.12.ids_ref, f32[128,256]{1,0:T(8,128)S(1)} %copy-done.5, ...), custom_call_target="tpu_custom_call" | custom-call | tf_op jit(solution)/shard_map/prepare/pallas_call | solution.py:251
  27.1 0.0 copy-start.3
  27.1 0.8 copy-done.3
  27.9 3.0 %collective-permute-start = (bf16[8,112,256]{2,1,0:T(8,128)(2,1)S(1)}, bf16[8,112,256]{2,1,0:T(8,128)(2,1)S(1)}, u32[]{:S(2)}, u32[]{:S(2)}) collective-permute-start(bf16[8,112,256]{2,1,0:T(8,128)(2,1)S(1)} %get-tuple-element.34), channel_id=1, source_target_pairs={{0,16},{16,0},{1,17},{17,1},{2,18},{18,2},{3,19},{19,3},{4,20},{20... | collective-permute-start | bytes 1376264 | tf_op jit(solution)/shard_map/ppermute | solution.py:303
  30.9 1.4 %collective-permute-done.other_ref = bf16[8,112,256]{2,1,0:T(8,128)(2,1)S(1)} collective-permute-done((bf16[8,112,256]{2,1,0:T(8,128)(2,1)S(1)}, bf16[8,112,256]{2,1,0:T(8,128)(2,1)S(1)}, u32[]{:S(2)}, u32[]{:S(2)}) %collective-permute-start) | collective-permute-done | bytes 458784 | tf_op jit(solution)/shard_map/ppermute | solution.py:303
  32.4 0.1 join.1
  32.4 7.1 %collective-permute-start.1 = (bf16[224,256]{1,0:T(8,128)(2,1)S(1)}, bf16[224,256]{1,0:T(8,128)(2,1)S(1)}, u32[]{:S(2)}, u32[]{:S(2)}) collective-permute-start(bf16[224,256]{1,0:T(8,128)(2,1)S(1)} %get-tuple-element.36), channel_id=1, source_target_pairs={{0,128},{32,160},{64,192},{96,224},{128,0},{160,32},{192,64},{224,... | collective-permute-start | bytes 344072 | tf_op jit(solution)/shard_map/ppermute | solution.py:307
  39.5 2.3 %collective-permute-start.2 = (bf16[224,256]{1,0:T(8,128)(2,1)S(1)}, bf16[224,256]{1,0:T(8,128)(2,1)S(1)}, u32[]{:S(2)}, u32[]{:S(2)}) collective-permute-start(bf16[224,256]{1,0:T(8,128)(2,1)S(1)} %get-tuple-element.37), channel_id=1, source_target_pairs={{0,96},{32,128},{64,160},{96,192},{128,224},{160,0},{192,32},{224,... | collective-permute-start | bytes 344072 | tf_op jit(solution)/shard_map/ppermute | solution.py:307
  41.8 6.0 %collective-permute-start.3 = (bf16[224,256]{1,0:T(8,128)(2,1)S(1)}, bf16[224,256]{1,0:T(8,128)(2,1)S(1)}, u32[]{:S(2)}, u32[]{:S(2)}) collective-permute-start(bf16[224,256]{1,0:T(8,128)(2,1)S(1)} %get-tuple-element.38), channel_id=1, source_target_pairs={{0,160},{32,192},{64,224},{96,0},{128,32},{160,64},{192,96},{224,1... | collective-permute-start | bytes 344072 | tf_op jit(solution)/shard_map/ppermute | solution.py:307
  47.8 2.2 %collective-permute-start.4 = (bf16[224,256]{1,0:T(8,128)(2,1)S(1)}, bf16[224,256]{1,0:T(8,128)(2,1)S(1)}, u32[]{:S(2)}, u32[]{:S(2)}) collective-permute-start(bf16[224,256]{1,0:T(8,128)(2,1)S(1)} %get-tuple-element.39), channel_id=1, source_target_pairs={{0,64},{32,96},{64,128},{96,160},{128,192},{160,224},{192,0},{224,... | collective-permute-start | bytes 344072 | tf_op jit(solution)/shard_map/ppermute | solution.py:307
  50.1 5.1 %collective-permute-start.5 = (bf16[224,256]{1,0:T(8,128)(2,1)S(1)}, bf16[224,256]{1,0:T(8,128)(2,1)S(1)}, u32[]{:S(2)}, u32[]{:S(2)}) collective-permute-start(bf16[224,256]{1,0:T(8,128)(2,1)S(1)} %get-tuple-element.40), channel_id=1, source_target_pairs={{0,192},{32,224},{64,0},{96,32},{128,64},{160,96},{192,128},{224,1... | collective-permute-start | bytes 344072 | tf_op jit(solution)/shard_map/ppermute | solution.py:307
  55.3 2.2 %collective-permute-start.6 = (bf16[224,256]{1,0:T(8,128)(2,1)S(1)}, bf16[224,256]{1,0:T(8,128)(2,1)S(1)}, u32[]{:S(2)}, u32[]{:S(2)}) collective-permute-start(bf16[224,256]{1,0:T(8,128)(2,1)S(1)} %get-tuple-element.41), channel_id=1, source_target_pairs={{0,32},{32,64},{64,96},{96,128},{128,160},{160,192},{192,224},{224... | collective-permute-start | bytes 344072 | tf_op jit(solution)/shard_map/ppermute | solution.py:307
  57.5 0.6 collective-permute-done.4.refs_4_
  58.1 3.9 %collective-permute-done.6.refs_6_ = bf16[224,256]{1,0:T(8,128)(2,1)S(1)} collective-permute-done((bf16[224,256]{1,0:T(8,128)(2,1)S(1)}, bf16[224,256]{1,0:T(8,128)(2,1)S(1)}, u32[]{:S(2)}, u32[]{:S(2)}) %collective-permute-start.6) | collective-permute-done | bytes 114720 | tf_op jit(solution)/shard_map/ppermute | solution.py:307
  62.0 1.4 %gate.1 = (f32[1,128]{1,0:T(1,128)}, f32[16,8,128]{2,1,0:T(8,128)}) custom-call(bf16[384,896]{1,0:T(8,128)(2,1)S(1)} %copy-done.4, bf16[384,1792]{1,0:T(8,128)(2,1)S(1)} %bitcast.12, bf16[384,384]{1,0:T(8,128)(2,1)S(1)} %copy-done, s32[8,128]{1,0:T(8,128)S(1)} %bitcast.16, s32[1,128]{1,0:T(1,128)S(1)} %bitcast.20), custom_call_target="tpu_custom_call" | custom-call | tf_op jit(solution)/shard_map/gate/pallas_call | solution.py:251
  63.4 6.2 %all-to-all-start.1 = ((f32[16,8,128]{2,1,0:T(8,128)}), f32[16,8,128]{2,1,0:T(8,128)S(1)}, u32[]{:S(2)}, u32[]{:S(2)}) async-start(f32[16,8,128]{2,1,0:T(8,128)} %get-tuple-element.44), calls=%async_computation.1 | async-start | bytes 131072 | tf_op jit(solution)/shard_map/all_to_all | solution.py:263
  69.6 4.6 %collective-permute-start.7 = (bf16[224,256]{1,0:T(8,128)(2,1)S(1)}, bf16[224,256]{1,0:T(8,128)(2,1)S(1)}, u32[]{:S(2)}, u32[]{:S(2)}) collective-permute-start(bf16[224,256]{1,0:T(8,128)(2,1)S(1)} %get-tuple-element.52), channel_id=1, source_target_pairs={{0,224},{32,0},{64,32},{96,64},{128,96},{160,128},{192,160},{224,1... | collective-permute-start | bytes 344072 | tf_op jit(solution)/shard_map/ppermute | solution.py:307
  74.2 2.4 %collective-permute-done.7.refs_7_ = bf16[224,256]{1,0:T(8,128)(2,1)S(1)} collective-permute-done((bf16[224,256]{1,0:T(8,128)(2,1)S(1)}, bf16[224,256]{1,0:T(8,128)(2,1)S(1)}, u32[]{:S(2)}, u32[]{:S(2)}) %collective-permute-start.7) | collective-permute-done | bytes 114720 | tf_op jit(solution)/shard_map/ppermute | solution.py:307
  76.6 0.8 all-to-all-done.1.gg_ref
  77.4 3.1 %contract.1 = bf16[64,8,128]{2,1,0:T(8,128)(2,1)} custom-call(s32[4]{0:T(128)S(1)} %pad_add_fusion.place_ref, f32[16,8,128]{2,1,0:T(8,128)S(1)} %all-to-all-done.1.gg_ref, s32[8,128]{1,0:T(8,128)S(1)} %bitcast.17, s32[1,128]{1,0:T(1,128)S(1)} %bitcast.21, bf16[224,256]{1,0:T(8,128)(2,1)S(1)} %get-tuple-element.45.refs_0_, ...), custom_call_target="tpu_custom_call" | custom-call | tf_op jit(solution)/shard_map/contract/pallas_call | solution.py:251
  80.5 12.7 %all-to-all-start.2 = ((bf16[64,8,128]{2,1,0:T(8,128)(2,1)}), bf16[64,8,128]{2,1,0:T(8,128)(2,1)S(1)}, u32[]{:S(2)}, u32[]{:S(2)}) async-start(bf16[64,8,128]{2,1,0:T(8,128)(2,1)} %contract.1), calls=%async_computation.2 | async-start | bytes 262144 | tf_op jit(solution)/shard_map/all_to_all | solution.py:263
  93.2 1.5 %unpack.1 = bf16[96,3584]{1,0:T(8,128)(2,1)} custom-call(bf16[384,1792]{1,0:T(8,128)(2,1)S(1)} %bitcast.13, bf16[384,384]{1,0:T(8,128)(2,1)S(1)} %copy-done), custom_call_target="tpu_custom_call" | custom-call | tf_op jit(solution)/shard_map/unpack/pallas_call | solution.py:251
  94.7 9.6 %all-to-all-done.2.far_ref = bf16[64,8,128]{2,1,0:T(8,128)(2,1)S(1)} async-done(((bf16[64,8,128]{2,1,0:T(8,128)(2,1)}), bf16[64,8,128]{2,1,0:T(8,128)(2,1)S(1)}, u32[]{:S(2)}, u32[]{:S(2)}) %all-to-all-start.2) | async-done | bytes 131104 | tf_op jit(solution)/shard_map/all_to_all | solution.py:263
  104.3 0.7 finish.1
  (15 shorter events, 0.0 us)
Async XLA Ops:
  4.4 18.7 %copy-start.6 = (s32[128,8]{0,1:T(8,128)S(1)}, s32[128,8]{0,1:T(8,128)}, u32[]{:S(2)}) copy-start(s32[128,8]{0,1:T(8,128)} %param.10) | copy-start | bytes 12292
  4.4 18.9 %copy-start = (bf16[384,384]{1,0:T(8,128)(2,1)S(1)}, bf16[384,384]{1,0:T(8,128)(2,1)}, u32[]{:S(2)}) copy-start(bf16[384,384]{1,0:T(8,128)(2,1)} %constant.26.clone.pack_hbm.pack_ref) | copy-start | bytes 884740
  4.4 18.9 %copy-start.1 = (bf16[128,3584]{1,0:T(8,128)(2,1)S(1)}, bf16[128,3584]{1,0:T(8,128)(2,1)}, u32[]{:S(2)}) copy-start(bf16[128,3584]{1,0:T(8,128)(2,1)} %og_ref.1) | copy-start | bytes 2752516
  4.4 18.9 %copy-start.2 = (bf16[96,3584]{1,0:T(8,128)(2,1)S(1)}, bf16[96,3584]{1,0:T(8,128)(2,1)}, u32[]{:S(2)}) copy-start(bf16[96,3584]{1,0:T(8,128)(2,1)} %get-tuple-element.31.deq_ref) | copy-start | bytes 2064388
  4.4 18.8 %copy-start.5 = (f32[128,256]{1,0:T(8,128)S(1)}, f32[128,256]{1,0:T(8,128)}, u32[]{:S(2)}) copy-start(f32[128,256]{1,0:T(8,128)} %logits_ref.1) | copy-start | bytes 393220
  4.4 18.8 %copy-start.7 = (s32[128]{0:T(128)S(1)}, s32[128]{0:T(128)}, u32[]{:S(2)}) copy-start(s32[128]{0:T(128)} %param.11) | copy-start | bytes 1540
  4.4 57.6 %all-to-all-start = ((bf16[16,24,1792]{2,1,0:T(8,128)(2,1)}), bf16[16,24,1792]{2,1,0:T(8,128)(2,1)S(1)}, u32[]{:S(2)}, u32[]{:S(2)}) async-start(bf16[16,24,1792]{2,1,0:T(8,128)(2,1)} %bitcast.22), calls=%async_computation | async-start | bytes 2752512 | tf_op jit(solution)/shard_map/all_to_all | solution.py:263
  27.1 0.8 copy-start.3
  27.9 34.1 %copy-start.4 = (bf16[384,896]{1,0:T(8,128)(2,1)S(1)}, bf16[384,896]{1,0:T(8,128)(2,1)}, u32[]{:S(2)}) copy-start(bf16[384,896]{1,0:T(8,128)(2,1)} %copy-done.3) | copy-start | bytes 2064388
  27.9 4.4 %collective-permute-start = (bf16[8,112,256]{2,1,0:T(8,128)(2,1)S(1)}, bf16[8,112,256]{2,1,0:T(8,128)(2,1)S(1)}, u32[]{:S(2)}, u32[]{:S(2)}) collective-permute-start(bf16[8,112,256]{2,1,0:T(8,128)(2,1)S(1)} %get-tuple-element.34), channel_id=1, source_target_pairs={{0,16},{16,0},{1,17},{17,1},{2,18},{18,2},{3,19},{19,3},{4,20},{20... | collective-permute-start | bytes 1376264 | tf_op jit(solution)/shard_map/ppermute | solution.py:303
  32.4 22.8 %collective-permute-start.1 = (bf16[224,256]{1,0:T(8,128)(2,1)S(1)}, bf16[224,256]{1,0:T(8,128)(2,1)S(1)}, u32[]{:S(2)}, u32[]{:S(2)}) collective-permute-start(bf16[224,256]{1,0:T(8,128)(2,1)S(1)} %get-tuple-element.36), channel_id=1, source_target_pairs={{0,128},{32,160},{64,192},{96,224},{128,0},{160,32},{192,64},{224,... | collective-permute-start | bytes 344072 | tf_op jit(solution)/shard_map/ppermute | solution.py:307
  39.5 18.0 %collective-permute-start.2 = (bf16[224,256]{1,0:T(8,128)(2,1)S(1)}, bf16[224,256]{1,0:T(8,128)(2,1)S(1)}, u32[]{:S(2)}, u32[]{:S(2)}) collective-permute-start(bf16[224,256]{1,0:T(8,128)(2,1)S(1)} %get-tuple-element.37), channel_id=1, source_target_pairs={{0,96},{32,128},{64,160},{96,192},{128,224},{160,0},{192,32},{224,... | collective-permute-start | bytes 344072 | tf_op jit(solution)/shard_map/ppermute | solution.py:307
  41.8 15.7 %collective-permute-start.3 = (bf16[224,256]{1,0:T(8,128)(2,1)S(1)}, bf16[224,256]{1,0:T(8,128)(2,1)S(1)}, u32[]{:S(2)}, u32[]{:S(2)}) collective-permute-start(bf16[224,256]{1,0:T(8,128)(2,1)S(1)} %get-tuple-element.38), channel_id=1, source_target_pairs={{0,160},{32,192},{64,224},{96,0},{128,32},{160,64},{192,96},{224,1... | collective-permute-start | bytes 344072 | tf_op jit(solution)/shard_map/ppermute | solution.py:307
  47.8 10.3 %collective-permute-start.4 = (bf16[224,256]{1,0:T(8,128)(2,1)S(1)}, bf16[224,256]{1,0:T(8,128)(2,1)S(1)}, u32[]{:S(2)}, u32[]{:S(2)}) collective-permute-start(bf16[224,256]{1,0:T(8,128)(2,1)S(1)} %get-tuple-element.39), channel_id=1, source_target_pairs={{0,64},{32,96},{64,128},{96,160},{128,192},{160,224},{192,0},{224,... | collective-permute-start | bytes 344072 | tf_op jit(solution)/shard_map/ppermute | solution.py:307
  50.1 8.1 %collective-permute-start.5 = (bf16[224,256]{1,0:T(8,128)(2,1)S(1)}, bf16[224,256]{1,0:T(8,128)(2,1)S(1)}, u32[]{:S(2)}, u32[]{:S(2)}) collective-permute-start(bf16[224,256]{1,0:T(8,128)(2,1)S(1)} %get-tuple-element.40), channel_id=1, source_target_pairs={{0,192},{32,224},{64,0},{96,32},{128,64},{160,96},{192,128},{224,1... | collective-permute-start | bytes 344072 | tf_op jit(solution)/shard_map/ppermute | solution.py:307
  55.3 6.7 %collective-permute-start.6 = (bf16[224,256]{1,0:T(8,128)(2,1)S(1)}, bf16[224,256]{1,0:T(8,128)(2,1)S(1)}, u32[]{:S(2)}, u32[]{:S(2)}) collective-permute-start(bf16[224,256]{1,0:T(8,128)(2,1)S(1)} %get-tuple-element.41), channel_id=1, source_target_pairs={{0,32},{32,64},{64,96},{96,128},{128,160},{160,192},{192,224},{224... | collective-permute-start | bytes 344072 | tf_op jit(solution)/shard_map/ppermute | solution.py:307
  63.4 14.1 %all-to-all-start.1 = ((f32[16,8,128]{2,1,0:T(8,128)}), f32[16,8,128]{2,1,0:T(8,128)S(1)}, u32[]{:S(2)}, u32[]{:S(2)}) async-start(f32[16,8,128]{2,1,0:T(8,128)} %get-tuple-element.44), calls=%async_computation.1 | async-start | bytes 131072 | tf_op jit(solution)/shard_map/all_to_all | solution.py:263
  69.6 7.0 %collective-permute-start.7 = (bf16[224,256]{1,0:T(8,128)(2,1)S(1)}, bf16[224,256]{1,0:T(8,128)(2,1)S(1)}, u32[]{:S(2)}, u32[]{:S(2)}) collective-permute-start(bf16[224,256]{1,0:T(8,128)(2,1)S(1)} %get-tuple-element.52), channel_id=1, source_target_pairs={{0,224},{32,0},{64,32},{96,64},{128,96},{160,128},{192,160},{224,1... | collective-permute-start | bytes 344072 | tf_op jit(solution)/shard_map/ppermute | solution.py:307
  80.5 23.8 %all-to-all-start.2 = ((bf16[64,8,128]{2,1,0:T(8,128)(2,1)}), bf16[64,8,128]{2,1,0:T(8,128)(2,1)S(1)}, u32[]{:S(2)}, u32[]{:S(2)}) async-start(bf16[64,8,128]{2,1,0:T(8,128)(2,1)} %contract.1), calls=%async_computation.2 | async-start | bytes 262144 | tf_op jit(solution)/shard_map/all_to_all | solution.py:263

commit v3 on v2

--- a/solution.py
+++ b/solution.py
@@ -99,12 +99,14 @@
     rows_out.wait()
 
 
-def prepare(place_ref, idt_ref, slots_ref, ids_ref, logits_ref, og_ref, deq_ref, pack_ref, og_hbm, own_out, other_out, og_out, og_sem):
+def grads(idt_ref, slots_ref, og_ref, pack_ref, og_out):
     pick = slot_matrix(idt_ref[0:1, :], slots_ref[...]).astype(bf16)
     og = dot(pick[:SLOTS], og_ref[...]).astype(bf16)
     og_out[...] = dot(pack_ref[...], stacked(og)).astype(bf16)
-    og_copy = pltpu.make_async_copy(og_out, og_hbm, og_sem)
-    og_copy.start()
+
+
+def prepare(place_ref, idt_ref, slots_ref, ids_ref, logits_ref, deq_ref, own_out, other_out):
+    pick = slot_matrix(idt_ref[0:1, :], slots_ref[...]).astype(bf16)
     logits = logits_ref[...]
     ids = ids_ref[...]
     wide_lane = lax.broadcasted_iota(jnp.int32, (TOK, EXPERTS), 1)
@@ -144,7 +146,6 @@
         other_out[step, :SLOTS, :] = jnp.where(core == 0, pieces[1], pieces[0])
         own_out[step, SLOTS:, :] = block
         other_out[step, SLOTS:, :] = block
-    og_copy.wait()
 
 
 def join(own_ref, other_ref, *outs):
@@ -186,18 +187,19 @@
     near_refs = refs[:RING]
     out_hbm, acc_ref, out_ref, out_sem = refs[RING:]
     yh, mine, x, core = (place_ref[n] for n in range(4))
-    rows = lax.broadcasted_iota(jnp.int32, (EXPERTS, TOK), 0).astype(f32)
+    rows = lax.broadcasted_iota(jnp.int32, (EXPERTS, TOK), 0).astype(f32).astype(bf16)
     for n, step in enumerate(STEPS):
         left = []
         for o in range(2):
             at = o * ROWS + SLOTS
             meta = near_refs[n][at : at + META, :].astype(f32)
             source = ((x - step) & (RING - 1)) * 2 + (core ^ o)
-            term = jnp.zeros((EXPERTS, TOK), f32)
+            term = jnp.zeros((EXPERTS, TOK), bf16)
             for k in range(TOPK):
                 coef = meta[k : k + 1, TOK:] + meta[8 + k : 9 + k, :TOK]
-                term = term + jnp.where(rows == meta[k : k + 1, :TOK], coef * gg_ref[source, 0:1, :], 0.0)
-            left.append(term.astype(bf16)[:, :ROWS])
+                value = (coef * gg_ref[source, 0:1, :]).astype(bf16)
+                term = jnp.where(rows == meta[k : k + 1, :TOK].astype(bf16), value, term)
+            left.append(term[:, :ROWS])
         part = dot(jnp.concatenate(left, axis=1), near_refs[n][...])
         if n == 0:
             acc_ref[...] = part
@@ -292,15 +294,16 @@
         limit=58,
     )
     got = swap(out, OWNERS)
-    og, own, other = call(
+    own, other = call(
         prepare,
-        [((PACKED, WIDE), bf16), ((RING, ROWS, 256), bf16), ((RING, ROWS, 256), bf16)],
-        (place, idt, slots, route_ids, router_logits, output_grad, deq, pack),
-        scratch=[pltpu.VMEM((PACKED, WIDE), bf16), pltpu.SemaphoreType.DMA],
+        [((RING, ROWS, 256), bf16), ((RING, ROWS, 256), bf16)],
+        (place, idt, slots, route_ids, router_logits, deq),
         scalars=1,
-        hbm_out=(0,),
-    )
+    )
+    own, other, output_grad = lax.optimization_barrier((own, other, output_grad))
+    (og,) = call(grads, [((PACKED, WIDE), bf16)], (idt, slots, output_grad, pack))
     other = lax.ppermute(other, "core", [(0, 1), (1, 0)])
+    other, og = lax.optimization_barrier((other, og))
     joined = call(join, [((2 * ROWS, 256), bf16)] * RING, (own, other))
     near = [joined[0]]
     for step in STEPS[1:]:

time: 107 us -> 104 us (0.972)
  Pallas kernels: 14.3 us -> 13.1 us
    pallas_call x7 -> x8, Pallas kernels: 14.3 us -> 13.1 us  [call(): pl.pallas_call(body, out_shape=[jax.ShapeDtypeStruct(s, t) for s, t in ou...]
where the time goes in v3:
time: 104 us; the launch traced here: 102 us
  starting transfers between devices  70 us (67%)
  waiting for transfers between devices  18 us (17%)
  Pallas kernels  13.1 us (13%)
    all_to_all x3, starting transfers between devices, swap(): return lax.all_to_all(v, axes, split_axis=0, concat_axis=0, tiled=True)  37.5 us
    ppermute x7, starting transfers between devices, shards(): lax.ppermute(joined[step], 'x', [(i, (i + step) % RING) for i in range(RI...  29.6 us
    pallas_call x8, Pallas kernels, call(): pl.pallas_call(body, out_shape=[jax.ShapeDtypeStruct(s, t) for s, t in ou...  13.1 us
    all_to_all x3, waiting for transfers between devices, swap(): return lax.all_to_all(v, axes, split_axis=0, concat_axis=0, tiled=True)  10.5 us
    ppermute x7, waiting for transfers between devices, shards(): lax.ppermute(joined[step], 'x', [(i, (i + step) % RING) for i in range(RI...  6.9 us
    ppermute x1, starting transfers between devices, shards(): other = lax.ppermute(other, 'core', [(0, 1), (1, 0)])  2.87 us
  transfers between devices with their start and end apart: 11, of which 6 were waited for; matrix products, arithmetic and copies ran while one was open for 0% of the time, Pallas kernels for 5%

profile of v3, /device:TPU:1, one launch (start us, length us, event | category | flops | bytes accessed | tf_op | source)
XLA Modules:
  0.0 102.0 jit_solution(12562602143794380899)
XLA Ops:
  0.6 3.7 %outgoing.1 = (bf16[384,1792]{1,0:T(8,128)(2,1)}, bf16[96,3584]{1,0:T(8,128)(2,1)}) custom-call(s32[8,128]{1,0:T(8,128)} %bitcast.14, s32[1,128]{1,0:T(1,128)} %bitcast.19, bf16[128,3584]{1,0:T(8,128)(2,1)} %tv_hbm.1, bf16[28,128]{1,0:T(8,128)(2,1)} %bitcast.25, bf16[96,3584]{1,0:T(8,128)(2,1)} %eo_hbm.1, bf16[384,384]{1,0:T(8,128)(2,1)} %constant.26.clone.pack_hbm.pack_ref), custom_call_target="tpu_custom_call" | custom-call | tf_op jit(solution)/shard_map/outgoing/pallas_call | solution.py:253
  4.4 0.0 copy-start.3
  4.4 0.0 copy-start.4
  4.4 0.0 copy-start.5
  4.4 0.0 copy-start
  4.4 0.0 copy-start.1
  4.5 18.6 %all-to-all-start = ((bf16[16,24,1792]{2,1,0:T(8,128)(2,1)}), bf16[16,24,1792]{2,1,0:T(8,128)(2,1)S(1)}, u32[]{:S(2)}, u32[]{:S(2)}) async-start(bf16[16,24,1792]{2,1,0:T(8,128)(2,1)} %bitcast.24), calls=%async_computation | async-start | bytes 2752512 | tf_op jit(solution)/shard_map/all_to_all | solution.py:265
  23.1 0.1 copy.12.ids_ref
  23.2 0.1 pad_add_fusion.place_ref
  23.3 2.7 %prepare.1 = (bf16[8,112,256]{2,1,0:T(8,128)(2,1)S(1)}, bf16[8,112,256]{2,1,0:T(8,128)(2,1)S(1)}) custom-call(s32[4]{0:T(128)S(1)} %pad_add_fusion.place_ref, s32[8,128]{1,0:T(8,128)S(1)} %bitcast.15, s32[1,128]{1,0:T(1,128)S(1)} %bitcast.20, s32[128,8]{1,0:T(8,128)S(1)} %copy.12.ids_ref, f32[128,256]{1,0:T(8,128)S(1)} %copy-done.4, ...), custom_call_target="tpu_custom_call" | custom-call | tf_op jit(solution)/shard_map/prepare/pallas_call | solution.py:253
  26.0 2.9 %collective-permute-start = (bf16[8,112,256]{2,1,0:T(8,128)(2,1)S(1)}, bf16[8,112,256]{2,1,0:T(8,128)(2,1)S(1)}, u32[]{:S(2)}, u32[]{:S(2)}) collective-permute-start(bf16[8,112,256]{2,1,0:T(8,128)(2,1)S(1)} %get-tuple-element.38), channel_id=1, source_target_pairs={{0,16},{16,0},{1,17},{17,1},{2,18},{18,2},{3,19},{19,3},{4,20},{20... | collective-permute-start | bytes 1376264 | tf_op jit(solution)/shard_map/ppermute | solution.py:305
  28.9 0.8 grads.1.og_ref
  29.7 0.6 collective-permute-done.other_ref
  30.3 0.1 join.1
  30.3 7.1 %collective-permute-start.1 = (bf16[224,256]{1,0:T(8,128)(2,1)S(1)}, bf16[224,256]{1,0:T(8,128)(2,1)S(1)}, u32[]{:S(2)}, u32[]{:S(2)}) collective-permute-start(bf16[224,256]{1,0:T(8,128)(2,1)S(1)} %get-tuple-element.44), channel_id=1, source_target_pairs={{0,128},{32,160},{64,192},{96,224},{128,0},{160,32},{192,64},{224,... | collective-permute-start | bytes 344072 | tf_op jit(solution)/shard_map/ppermute | solution.py:310
  37.5 2.3 %collective-permute-start.2 = (bf16[224,256]{1,0:T(8,128)(2,1)S(1)}, bf16[224,256]{1,0:T(8,128)(2,1)S(1)}, u32[]{:S(2)}, u32[]{:S(2)}) collective-permute-start(bf16[224,256]{1,0:T(8,128)(2,1)S(1)} %get-tuple-element.45), channel_id=1, source_target_pairs={{0,96},{32,128},{64,160},{96,192},{128,224},{160,0},{192,32},{224,... | collective-permute-start | bytes 344072 | tf_op jit(solution)/shard_map/ppermute | solution.py:310
  39.8 6.0 %collective-permute-start.3 = (bf16[224,256]{1,0:T(8,128)(2,1)S(1)}, bf16[224,256]{1,0:T(8,128)(2,1)S(1)}, u32[]{:S(2)}, u32[]{:S(2)}) collective-permute-start(bf16[224,256]{1,0:T(8,128)(2,1)S(1)} %get-tuple-element.46), channel_id=1, source_target_pairs={{0,160},{32,192},{64,224},{96,0},{128,32},{160,64},{192,96},{224,1... | collective-permute-start | bytes 344072 | tf_op jit(solution)/shard_map/ppermute | solution.py:310
  45.8 2.2 %collective-permute-start.4 = (bf16[224,256]{1,0:T(8,128)(2,1)S(1)}, bf16[224,256]{1,0:T(8,128)(2,1)S(1)}, u32[]{:S(2)}, u32[]{:S(2)}) collective-permute-start(bf16[224,256]{1,0:T(8,128)(2,1)S(1)} %get-tuple-element.47), channel_id=1, source_target_pairs={{0,64},{32,96},{64,128},{96,160},{128,192},{160,224},{192,0},{224,... | collective-permute-start | bytes 344072 | tf_op jit(solution)/shard_map/ppermute | solution.py:310
  48.0 5.1 %collective-permute-start.5 = (bf16[224,256]{1,0:T(8,128)(2,1)S(1)}, bf16[224,256]{1,0:T(8,128)(2,1)S(1)}, u32[]{:S(2)}, u32[]{:S(2)}) collective-permute-start(bf16[224,256]{1,0:T(8,128)(2,1)S(1)} %get-tuple-element.48), channel_id=1, source_target_pairs={{0,192},{32,224},{64,0},{96,32},{128,64},{160,96},{192,128},{224,1... | collective-permute-start | bytes 344072 | tf_op jit(solution)/shard_map/ppermute | solution.py:310
  53.2 2.2 %collective-permute-start.6 = (bf16[224,256]{1,0:T(8,128)(2,1)S(1)}, bf16[224,256]{1,0:T(8,128)(2,1)S(1)}, u32[]{:S(2)}, u32[]{:S(2)}) collective-permute-start(bf16[224,256]{1,0:T(8,128)(2,1)S(1)} %get-tuple-element.49), channel_id=1, source_target_pairs={{0,32},{32,64},{64,96},{96,128},{128,160},{160,192},{192,224},{224... | collective-permute-start | bytes 344072 | tf_op jit(solution)/shard_map/ppermute | solution.py:310
  55.5 0.6 collective-permute-done.4.refs_4_
  56.1 3.8 %collective-permute-done.6.refs_6_ = bf16[224,256]{1,0:T(8,128)(2,1)S(1)} collective-permute-done((bf16[224,256]{1,0:T(8,128)(2,1)S(1)}, bf16[224,256]{1,0:T(8,128)(2,1)S(1)}, u32[]{:S(2)}, u32[]{:S(2)}) %collective-permute-start.6) | collective-permute-done | bytes 114720 | tf_op jit(solution)/shard_map/ppermute | solution.py:310
  59.9 1.4 %gate.1 = (f32[1,128]{1,0:T(1,128)}, f32[16,8,128]{2,1,0:T(8,128)}) custom-call(bf16[384,896]{1,0:T(8,128)(2,1)S(1)} %grads.1.og_ref, bf16[384,1792]{1,0:T(8,128)(2,1)S(1)} %bitcast.12, bf16[384,384]{1,0:T(8,128)(2,1)S(1)} %copy-done, s32[8,128]{1,0:T(8,128)S(1)} %bitcast.17, s32[1,128]{1,0:T(1,128)S(1)} %bitcast.22), custom_call_target="tpu_custom_call" | custom-call | tf_op jit(solution)/shard_map/gate/pallas_call | solution.py:253
  61.3 6.2 %all-to-all-start.1 = ((f32[16,8,128]{2,1,0:T(8,128)}), f32[16,8,128]{2,1,0:T(8,128)S(1)}, u32[]{:S(2)}, u32[]{:S(2)}) async-start(f32[16,8,128]{2,1,0:T(8,128)} %get-tuple-element.52), calls=%async_computation.1 | async-start | bytes 131072 | tf_op jit(solution)/shard_map/all_to_all | solution.py:265
  67.5 4.6 %collective-permute-start.7 = (bf16[224,256]{1,0:T(8,128)(2,1)S(1)}, bf16[224,256]{1,0:T(8,128)(2,1)S(1)}, u32[]{:S(2)}, u32[]{:S(2)}) collective-permute-start(bf16[224,256]{1,0:T(8,128)(2,1)S(1)} %get-tuple-element.60), channel_id=1, source_target_pairs={{0,224},{32,0},{64,32},{96,64},{128,96},{160,128},{192,160},{224,1... | collective-permute-start | bytes 344072 | tf_op jit(solution)/shard_map/ppermute | solution.py:310
  72.1 2.4 %collective-permute-done.7.refs_7_ = bf16[224,256]{1,0:T(8,128)(2,1)S(1)} collective-permute-done((bf16[224,256]{1,0:T(8,128)(2,1)S(1)}, bf16[224,256]{1,0:T(8,128)(2,1)S(1)}, u32[]{:S(2)}, u32[]{:S(2)}) %collective-permute-start.7) | collective-permute-done | bytes 114720 | tf_op jit(solution)/shard_map/ppermute | solution.py:310
  74.5 0.8 all-to-all-done.1.gg_ref
  75.4 2.1 %contract.1 = bf16[64,8,128]{2,1,0:T(8,128)(2,1)} custom-call(s32[4]{0:T(128)S(1)} %pad_add_fusion.place_ref, f32[16,8,128]{2,1,0:T(8,128)S(1)} %all-to-all-done.1.gg_ref, s32[8,128]{1,0:T(8,128)S(1)} %bitcast.18, s32[1,128]{1,0:T(1,128)S(1)} %bitcast.23, bf16[224,256]{1,0:T(8,128)(2,1)S(1)} %get-tuple-element.53.refs_0_, ...), custom_call_target="tpu_custom_call" | custom-call | tf_op jit(solution)/shard_map/contract/pallas_call | solution.py:253
  77.5 12.7 %all-to-all-start.2 = ((bf16[64,8,128]{2,1,0:T(8,128)(2,1)}), bf16[64,8,128]{2,1,0:T(8,128)(2,1)S(1)}, u32[]{:S(2)}, u32[]{:S(2)}) async-start(bf16[64,8,128]{2,1,0:T(8,128)(2,1)} %contract.1), calls=%async_computation.2 | async-start | bytes 262144 | tf_op jit(solution)/shard_map/all_to_all | solution.py:265
  90.1 1.5 %unpack.1 = bf16[96,3584]{1,0:T(8,128)(2,1)} custom-call(bf16[384,1792]{1,0:T(8,128)(2,1)S(1)} %bitcast.13, bf16[384,384]{1,0:T(8,128)(2,1)S(1)} %copy-done), custom_call_target="tpu_custom_call" | custom-call | tf_op jit(solution)/shard_map/unpack/pallas_call | solution.py:253
  91.7 9.6 %all-to-all-done.2.far_ref = bf16[64,8,128]{2,1,0:T(8,128)(2,1)S(1)} async-done(((bf16[64,8,128]{2,1,0:T(8,128)(2,1)}), bf16[64,8,128]{2,1,0:T(8,128)(2,1)S(1)}, u32[]{:S(2)}, u32[]{:S(2)}) %all-to-all-start.2) | async-done | bytes 131104 | tf_op jit(solution)/shard_map/all_to_all | solution.py:265
  101.3 0.7 finish.1
  (12 shorter events, 0.0 us)
Async XLA Ops:
  4.4 18.7 %copy-start.3 = (s32[128,8]{0,1:T(8,128)S(1)}, s32[128,8]{0,1:T(8,128)}, u32[]{:S(2)}) copy-start(s32[128,8]{0,1:T(8,128)} %param.10) | copy-start | bytes 12292
  4.4 18.9 %copy-start.2 = (bf16[96,3584]{1,0:T(8,128)(2,1)S(1)}, bf16[96,3584]{1,0:T(8,128)(2,1)}, u32[]{:S(2)}) copy-start(bf16[96,3584]{1,0:T(8,128)(2,1)} %get-tuple-element.35.deq_ref) | copy-start | bytes 2064388
  4.4 18.9 %copy-start.4 = (f32[128,256]{1,0:T(8,128)S(1)}, f32[128,256]{1,0:T(8,128)}, u32[]{:S(2)}) copy-start(f32[128,256]{1,0:T(8,128)} %logits_ref.1) | copy-start | bytes 393220
  4.4 18.9 %copy-start.5 = (s32[128]{0:T(128)S(1)}, s32[128]{0:T(128)}, u32[]{:S(2)}) copy-start(s32[128]{0:T(128)} %param.11) | copy-start | bytes 1540
  4.4 24.4 %copy-start = (bf16[384,384]{1,0:T(8,128)(2,1)S(1)}, bf16[384,384]{1,0:T(8,128)(2,1)}, u32[]{:S(2)}) copy-start(bf16[384,384]{1,0:T(8,128)(2,1)} %constant.26.clone.pack_hbm.pack_ref) | copy-start | bytes 884740
  4.4 24.4 %copy-start.1 = (bf16[128,3584]{1,0:T(8,128)(2,1)S(1)}, bf16[128,3584]{1,0:T(8,128)(2,1)}, u32[]{:S(2)}) copy-start(bf16[128,3584]{1,0:T(8,128)(2,1)} %og_ref) | copy-start | bytes 2752516
  4.5 55.5 %all-to-all-start = ((bf16[16,24,1792]{2,1,0:T(8,128)(2,1)}), bf16[16,24,1792]{2,1,0:T(8,128)(2,1)S(1)}, u32[]{:S(2)}, u32[]{:S(2)}) async-start(bf16[16,24,1792]{2,1,0:T(8,128)(2,1)} %bitcast.24), calls=%async_computation | async-start | bytes 2752512 | tf_op jit(solution)/shard_map/all_to_all | solution.py:265
  26.0 4.3 %collective-permute-start = (bf16[8,112,256]{2,1,0:T(8,128)(2,1)S(1)}, bf16[8,112,256]{2,1,0:T(8,128)(2,1)S(1)}, u32[]{:S(2)}, u32[]{:S(2)}) collective-permute-start(bf16[8,112,256]{2,1,0:T(8,128)(2,1)S(1)} %get-tuple-element.38), channel_id=1, source_target_pairs={{0,16},{16,0},{1,17},{17,1},{2,18},{18,2},{3,19},{19,3},{4,20},{20... | collective-permute-start | bytes 1376264 | tf_op jit(solution)/shard_map/ppermute | solution.py:305
  30.3 22.8 %collective-permute-start.1 = (bf16[224,256]{1,0:T(8,128)(2,1)S(1)}, bf16[224,256]{1,0:T(8,128)(2,1)S(1)}, u32[]{:S(2)}, u32[]{:S(2)}) collective-permute-start(bf16[224,256]{1,0:T(8,128)(2,1)S(1)} %get-tuple-element.44), channel_id=1, source_target_pairs={{0,128},{32,160},{64,192},{96,224},{128,0},{160,32},{192,64},{224,... | collective-permute-start | bytes 344072 | tf_op jit(solution)/shard_map/ppermute | solution.py:310
  37.5 18.0 %collective-permute-start.2 = (bf16[224,256]{1,0:T(8,128)(2,1)S(1)}, bf16[224,256]{1,0:T(8,128)(2,1)S(1)}, u32[]{:S(2)}, u32[]{:S(2)}) collective-permute-start(bf16[224,256]{1,0:T(8,128)(2,1)S(1)} %get-tuple-element.45), channel_id=1, source_target_pairs={{0,96},{32,128},{64,160},{96,192},{128,224},{160,0},{192,32},{224,... | collective-permute-start | bytes 344072 | tf_op jit(solution)/shard_map/ppermute | solution.py:310
  39.8 15.7 %collective-permute-start.3 = (bf16[224,256]{1,0:T(8,128)(2,1)S(1)}, bf16[224,256]{1,0:T(8,128)(2,1)S(1)}, u32[]{:S(2)}, u32[]{:S(2)}) collective-permute-start(bf16[224,256]{1,0:T(8,128)(2,1)S(1)} %get-tuple-element.46), channel_id=1, source_target_pairs={{0,160},{32,192},{64,224},{96,0},{128,32},{160,64},{192,96},{224,1... | collective-permute-start | bytes 344072 | tf_op jit(solution)/shard_map/ppermute | solution.py:310
  45.8 10.3 %collective-permute-start.4 = (bf16[224,256]{1,0:T(8,128)(2,1)S(1)}, bf16[224,256]{1,0:T(8,128)(2,1)S(1)}, u32[]{:S(2)}, u32[]{:S(2)}) collective-permute-start(bf16[224,256]{1,0:T(8,128)(2,1)S(1)} %get-tuple-element.47), channel_id=1, source_target_pairs={{0,64},{32,96},{64,128},{96,160},{128,192},{160,224},{192,0},{224,... | collective-permute-start | bytes 344072 | tf_op jit(solution)/shard_map/ppermute | solution.py:310
  48.0 8.1 %collective-permute-start.5 = (bf16[224,256]{1,0:T(8,128)(2,1)S(1)}, bf16[224,256]{1,0:T(8,128)(2,1)S(1)}, u32[]{:S(2)}, u32[]{:S(2)}) collective-permute-start(bf16[224,256]{1,0:T(8,128)(2,1)S(1)} %get-tuple-element.48), channel_id=1, source_target_pairs={{0,192},{32,224},{64,0},{96,32},{128,64},{160,96},{192,128},{224,1... | collective-permute-start | bytes 344072 | tf_op jit(solution)/shard_map/ppermute | solution.py:310
  53.2 6.7 %collective-permute-start.6 = (bf16[224,256]{1,0:T(8,128)(2,1)S(1)}, bf16[224,256]{1,0:T(8,128)(2,1)S(1)}, u32[]{:S(2)}, u32[]{:S(2)}) collective-permute-start(bf16[224,256]{1,0:T(8,128)(2,1)S(1)} %get-tuple-element.49), channel_id=1, source_target_pairs={{0,32},{32,64},{64,96},{96,128},{128,160},{160,192},{192,224},{224... | collective-permute-start | bytes 344072 | tf_op jit(solution)/shard_map/ppermute | solution.py:310
  61.3 14.1 %all-to-all-start.1 = ((f32[16,8,128]{2,1,0:T(8,128)}), f32[16,8,128]{2,1,0:T(8,128)S(1)}, u32[]{:S(2)}, u32[]{:S(2)}) async-start(f32[16,8,128]{2,1,0:T(8,128)} %get-tuple-element.52), calls=%async_computation.1 | async-start | bytes 131072 | tf_op jit(solution)/shard_map/all_to_all | solution.py:265
  67.5 7.0 %collective-permute-start.7 = (bf16[224,256]{1,0:T(8,128)(2,1)S(1)}, bf16[224,256]{1,0:T(8,128)(2,1)S(1)}, u32[]{:S(2)}, u32[]{:S(2)}) collective-permute-start(bf16[224,256]{1,0:T(8,128)(2,1)S(1)} %get-tuple-element.60), channel_id=1, source_target_pairs={{0,224},{32,0},{64,32},{96,64},{128,96},{160,128},{192,160},{224,1... | collective-permute-start | bytes 344072 | tf_op jit(solution)/shard_map/ppermute | solution.py:310
  77.5 23.8 %all-to-all-start.2 = ((bf16[64,8,128]{2,1,0:T(8,128)(2,1)}), bf16[64,8,128]{2,1,0:T(8,128)(2,1)S(1)}, u32[]{:S(2)}, u32[]{:S(2)}) async-start(bf16[64,8,128]{2,1,0:T(8,128)(2,1)} %contract.1), calls=%async_computation.2 | async-start | bytes 262144 | tf_op jit(solution)/shard_map/all_to_all | solution.py:265

commit v4 on v3

--- a/solution.py
+++ b/solution.py
@@ -171,7 +171,7 @@
     row = jnp.broadcast_to(row, (8, TOK))
     pick = slot_matrix(idt_ref[0:1, :], slots_ref[...])
     gate_ref[...] = dot(row, pick, precision=lax.Precision.HIGHEST)[0:1]
-    send_ref[...] = jnp.broadcast_to(row[None], (PEERS, 8, TOK))
+    send_ref[...] = jnp.broadcast_to(row[None, 0:1], (PEERS, 1, TOK))
 
 
 def unpack(got_ref, pack_ref, out_ref):
@@ -310,7 +310,7 @@
         near.append(lax.ppermute(joined[step], "x", [(i, (i + step) % RING) for i in range(RING)]))
     got, og, *near[:HELD] = lax.optimization_barrier((got, og, *near[:HELD]))
     gates, send = call(
-        gate, [((1, TOK), f32), ((PEERS, 8, TOK), f32)], (og, got, pack, idt, slots)
+        gate, [((1, TOK), f32), ((PEERS, 1, TOK), f32)], (og, got, pack, idt, slots)
     )
     gg = swap(send, NEAR)
     (expert_inputs,) = call(unpack, [((SLOTS, D), bf16)], (got, pack))

time: 104 us -> 102 us (0.981)
    ppermute x7, waiting for transfers between devices: 6.9 us -> 0.21 us  [shards(): lax.ppermute(joined[step], 'x', [(i, (i + step) % RING) for i in range(RI...]
    all_to_all x3, waiting for transfers between devices: 10.5 us -> 16.6 us  [swap(): return lax.all_to_all(v, axes, split_axis=0, concat_axis=0, tiled=True)]
  transfers between devices with their start and end apart: 11 -> 11, of which waited for: 6 -> 4; matrix products, arithmetic and copies ran while one was open for 0% -> 0% of each run, Pallas kernels for 5% -> 6%
where the time goes in v4:
time: 102 us; the launch traced here: 101 us
  starting transfers between devices  69.6 us (68%)
  waiting for transfers between devices  17.4 us (17%)
  Pallas kernels  13 us (13%)
    all_to_all x3, starting transfers between devices, swap(): return lax.all_to_all(v, axes, split_axis=0, concat_axis=0, tiled=True)  37.5 us
    ppermute x7, starting transfers between devices, shards(): lax.ppermute(joined[step], 'x', [(i, (i + step) % RING) for i in range(RI...  29.3 us
    all_to_all x3, waiting for transfers between devices, swap(): return lax.all_to_all(v, axes, split_axis=0, concat_axis=0, tiled=True)  16.6 us
    pallas_call x8, Pallas kernels, call(): pl.pallas_call(body, out_shape=[jax.ShapeDtypeStruct(s, t) for s, t in ou...  13 us
    ppermute x1, starting transfers between devices, shards(): other = lax.ppermute(other, 'core', [(0, 1), (1, 0)])  2.87 us
  transfers between devices with their start and end apart: 11, of which 4 were waited for; matrix products, arithmetic and copies ran while one was open for 0% of the time, Pallas kernels for 6%

profile of v4, /device:TPU:1, one launch (start us, length us, event | category | flops | bytes accessed | tf_op | source)
XLA Modules:
  0.0 101.0 jit_solution(15025599644513366610)
XLA Ops:
  0.6 3.7 %outgoing.1 = (bf16[384,1792]{1,0:T(8,128)(2,1)}, bf16[96,3584]{1,0:T(8,128)(2,1)}) custom-call(s32[8,128]{1,0:T(8,128)} %bitcast.14, s32[1,128]{1,0:T(1,128)} %bitcast.19, bf16[128,3584]{1,0:T(8,128)(2,1)} %tv_hbm.1, bf16[28,128]{1,0:T(8,128)(2,1)} %bitcast.25, bf16[96,3584]{1,0:T(8,128)(2,1)} %eo_hbm.1, bf16[384,384]{1,0:T(8,128)(2,1)} %constant.26.clone.pack_hbm.pack_ref), custom_call_target="tpu_custom_call" | custom-call | tf_op jit(solution)/shard_map/outgoing/pallas_call | solution.py:253
  4.4 0.0 copy-start.3
  4.4 0.0 copy-start.2
  4.4 0.0 copy-start.4
  4.4 0.0 copy-start.5
  4.4 0.0 copy-start
  4.4 0.0 copy-start.1
  4.5 18.6 %all-to-all-start = ((bf16[16,24,1792]{2,1,0:T(8,128)(2,1)}), bf16[16,24,1792]{2,1,0:T(8,128)(2,1)S(1)}, u32[]{:S(2)}, u32[]{:S(2)}) async-start(bf16[16,24,1792]{2,1,0:T(8,128)(2,1)} %bitcast.24), calls=%async_computation | async-start | bytes 2752512 | tf_op jit(solution)/shard_map/all_to_all | solution.py:265
  23.1 0.1 copy.12.ids_ref
  23.2 0.1 pad_add_fusion.place_ref
  23.3 2.7 %prepare.1 = (bf16[8,112,256]{2,1,0:T(8,128)(2,1)S(1)}, bf16[8,112,256]{2,1,0:T(8,128)(2,1)S(1)}) custom-call(s32[4]{0:T(128)S(1)} %pad_add_fusion.place_ref, s32[8,128]{1,0:T(8,128)S(1)} %bitcast.15, s32[1,128]{1,0:T(1,128)S(1)} %bitcast.20, s32[128,8]{1,0:T(8,128)S(1)} %copy.12.ids_ref, f32[128,256]{1,0:T(8,128)S(1)} %copy-done.4, ...), custom_call_target="tpu_custom_call" | custom-call | tf_op jit(solution)/shard_map/prepare/pallas_call | solution.py:253
  26.0 2.9 %collective-permute-start = (bf16[8,112,256]{2,1,0:T(8,128)(2,1)S(1)}, bf16[8,112,256]{2,1,0:T(8,128)(2,1)S(1)}, u32[]{:S(2)}, u32[]{:S(2)}) collective-permute-start(bf16[8,112,256]{2,1,0:T(8,128)(2,1)S(1)} %get-tuple-element.38), channel_id=1, source_target_pairs={{0,16},{16,0},{1,17},{17,1},{2,18},{18,2},{3,19},{19,3},{4,20},{20... | collective-permute-start | bytes 1376264 | tf_op jit(solution)/shard_map/ppermute | solution.py:305
  28.9 0.8 grads.1.og_ref
  29.7 0.6 collective-permute-done.other_ref
  30.3 0.1 join.1
  30.3 7.1 %collective-permute-start.1 = (bf16[224,256]{1,0:T(8,128)(2,1)S(1)}, bf16[224,256]{1,0:T(8,128)(2,1)S(1)}, u32[]{:S(2)}, u32[]{:S(2)}) collective-permute-start(bf16[224,256]{1,0:T(8,128)(2,1)S(1)} %get-tuple-element.44), channel_id=1, source_target_pairs={{0,128},{32,160},{64,192},{96,224},{128,0},{160,32},{192,64},{224,... | collective-permute-start | bytes 344072 | tf_op jit(solution)/shard_map/ppermute | solution.py:310
  37.5 2.3 %collective-permute-start.2 = (bf16[224,256]{1,0:T(8,128)(2,1)S(1)}, bf16[224,256]{1,0:T(8,128)(2,1)S(1)}, u32[]{:S(2)}, u32[]{:S(2)}) collective-permute-start(bf16[224,256]{1,0:T(8,128)(2,1)S(1)} %get-tuple-element.45), channel_id=1, source_target_pairs={{0,96},{32,128},{64,160},{96,192},{128,224},{160,0},{192,32},{224,... | collective-permute-start | bytes 344072 | tf_op jit(solution)/shard_map/ppermute | solution.py:310
  39.8 6.0 %collective-permute-start.3 = (bf16[224,256]{1,0:T(8,128)(2,1)S(1)}, bf16[224,256]{1,0:T(8,128)(2,1)S(1)}, u32[]{:S(2)}, u32[]{:S(2)}) collective-permute-start(bf16[224,256]{1,0:T(8,128)(2,1)S(1)} %get-tuple-element.46), channel_id=1, source_target_pairs={{0,160},{32,192},{64,224},{96,0},{128,32},{160,64},{192,96},{224,1... | collective-permute-start | bytes 344072 | tf_op jit(solution)/shard_map/ppermute | solution.py:310
  45.8 2.2 %collective-permute-start.4 = (bf16[224,256]{1,0:T(8,128)(2,1)S(1)}, bf16[224,256]{1,0:T(8,128)(2,1)S(1)}, u32[]{:S(2)}, u32[]{:S(2)}) collective-permute-start(bf16[224,256]{1,0:T(8,128)(2,1)S(1)} %get-tuple-element.47), channel_id=1, source_target_pairs={{0,64},{32,96},{64,128},{96,160},{128,192},{160,224},{192,0},{224,... | collective-permute-start | bytes 344072 | tf_op jit(solution)/shard_map/ppermute | solution.py:310
  48.0 5.1 %collective-permute-start.5 = (bf16[224,256]{1,0:T(8,128)(2,1)S(1)}, bf16[224,256]{1,0:T(8,128)(2,1)S(1)}, u32[]{:S(2)}, u32[]{:S(2)}) collective-permute-start(bf16[224,256]{1,0:T(8,128)(2,1)S(1)} %get-tuple-element.48), channel_id=1, source_target_pairs={{0,192},{32,224},{64,0},{96,32},{128,64},{160,96},{192,128},{224,1... | collective-permute-start | bytes 344072 | tf_op jit(solution)/shard_map/ppermute | solution.py:310
  53.2 0.0 collective-permute-done.1.refs_1_
  53.2 2.2 %collective-permute-start.6 = (bf16[224,256]{1,0:T(8,128)(2,1)S(1)}, bf16[224,256]{1,0:T(8,128)(2,1)S(1)}, u32[]{:S(2)}, u32[]{:S(2)}) collective-permute-start(bf16[224,256]{1,0:T(8,128)(2,1)S(1)} %get-tuple-element.49), channel_id=1, source_target_pairs={{0,32},{32,64},{64,96},{96,128},{128,160},{160,192},{192,224},{224... | collective-permute-start | bytes 344072 | tf_op jit(solution)/shard_map/ppermute | solution.py:310
  55.4 4.3 %collective-permute-start.7 = (bf16[224,256]{1,0:T(8,128)(2,1)S(1)}, bf16[224,256]{1,0:T(8,128)(2,1)S(1)}, u32[]{:S(2)}, u32[]{:S(2)}) collective-permute-start(bf16[224,256]{1,0:T(8,128)(2,1)S(1)} %get-tuple-element.60), channel_id=1, source_target_pairs={{0,224},{32,0},{64,32},{96,64},{128,96},{160,128},{192,160},{224,1... | collective-permute-start | bytes 344072 | tf_op jit(solution)/shard_map/ppermute | solution.py:310
  59.7 0.2 collective-permute-done.6.refs_6_
  59.9 1.4 %gate.1 = (f32[1,128]{1,0:T(1,128)}, f32[16,1,128]{2,1,0:T(1,128)}) custom-call(bf16[384,896]{1,0:T(8,128)(2,1)S(1)} %grads.1.og_ref, bf16[384,1792]{1,0:T(8,128)(2,1)S(1)} %bitcast.12, bf16[384,384]{1,0:T(8,128)(2,1)S(1)} %copy-done, s32[8,128]{1,0:T(8,128)S(1)} %bitcast.17, s32[1,128]{1,0:T(1,128)S(1)} %bitcast.22), custom_call_target="tpu_custom_call" | custom-call | tf_op jit(solution)/shard_map/gate/pallas_call | solution.py:253
  61.3 6.2 %all-to-all-start.1 = ((f32[16,1,128]{2,1,0:T(1,128)}), f32[16,1,128]{2,1,0:T(1,128)S(1)}, u32[]{:S(2)}, u32[]{:S(2)}) async-start(f32[16,1,128]{2,1,0:T(1,128)} %get-tuple-element.52), calls=%async_computation.1 | async-start | bytes 16384 | tf_op jit(solution)/shard_map/all_to_all | solution.py:265
  67.5 7.0 %all-to-all-done.1.gg_ref = f32[16,1,128]{2,1,0:T(1,128)S(1)} async-done(((f32[16,1,128]{2,1,0:T(1,128)}), f32[16,1,128]{2,1,0:T(1,128)S(1)}, u32[]{:S(2)}, u32[]{:S(2)}) %all-to-all-start.1) | async-done | bytes 8224 | tf_op jit(solution)/shard_map/all_to_all | solution.py:265
  74.5 2.0 %contract.1 = bf16[64,8,128]{2,1,0:T(8,128)(2,1)} custom-call(s32[4]{0:T(128)S(1)} %pad_add_fusion.place_ref, f32[16,1,128]{2,1,0:T(1,128)S(1)} %all-to-all-done.1.gg_ref, s32[8,128]{1,0:T(8,128)S(1)} %bitcast.18, s32[1,128]{1,0:T(1,128)S(1)} %bitcast.23, bf16[224,256]{1,0:T(8,128)(2,1)S(1)} %get-tuple-element.53.refs_0_, ...), custom_call_target="tpu_custom_call" | custom-call | tf_op jit(solution)/shard_map/contract/pallas_call | solution.py:253
  76.5 12.7 %all-to-all-start.2 = ((bf16[64,8,128]{2,1,0:T(8,128)(2,1)}), bf16[64,8,128]{2,1,0:T(8,128)(2,1)S(1)}, u32[]{:S(2)}, u32[]{:S(2)}) async-start(bf16[64,8,128]{2,1,0:T(8,128)(2,1)} %contract.1), calls=%async_computation.2 | async-start | bytes 262144 | tf_op jit(solution)/shard_map/all_to_all | solution.py:265
  89.2 1.5 %unpack.1 = bf16[96,3584]{1,0:T(8,128)(2,1)} custom-call(bf16[384,1792]{1,0:T(8,128)(2,1)S(1)} %bitcast.13, bf16[384,384]{1,0:T(8,128)(2,1)S(1)} %copy-done), custom_call_target="tpu_custom_call" | custom-call | tf_op jit(solution)/shard_map/unpack/pallas_call | solution.py:253
  90.7 9.6 %all-to-all-done.2.far_ref = bf16[64,8,128]{2,1,0:T(8,128)(2,1)S(1)} async-done(((bf16[64,8,128]{2,1,0:T(8,128)(2,1)}), bf16[64,8,128]{2,1,0:T(8,128)(2,1)S(1)}, u32[]{:S(2)}, u32[]{:S(2)}) %all-to-all-start.2) | async-done | bytes 131104 | tf_op jit(solution)/shard_map/all_to_all | solution.py:265
  100.3 0.7 finish.1
  (12 shorter events, 0.0 us)
Async XLA Ops:
  4.4 18.7 %copy-start.3 = (s32[128,8]{0,1:T(8,128)S(1)}, s32[128,8]{0,1:T(8,128)}, u32[]{:S(2)}) copy-start(s32[128,8]{0,1:T(8,128)} %param.10) | copy-start | bytes 12292
  4.4 18.9 %copy-start.2 = (bf16[96,3584]{1,0:T(8,128)(2,1)S(1)}, bf16[96,3584]{1,0:T(8,128)(2,1)}, u32[]{:S(2)}) copy-start(bf16[96,3584]{1,0:T(8,128)(2,1)} %get-tuple-element.35.deq_ref) | copy-start | bytes 2064388
  4.4 18.9 %copy-start.4 = (f32[128,256]{1,0:T(8,128)S(1)}, f32[128,256]{1,0:T(8,128)}, u32[]{:S(2)}) copy-start(f32[128,256]{1,0:T(8,128)} %logits_ref.1) | copy-start | bytes 393220
  4.4 18.9 %copy-start.5 = (s32[128]{0:T(128)S(1)}, s32[128]{0:T(128)}, u32[]{:S(2)}) copy-start(s32[128]{0:T(128)} %param.11) | copy-start | bytes 1540
  4.4 24.4 %copy-start = (bf16[384,384]{1,0:T(8,128)(2,1)S(1)}, bf16[384,384]{1,0:T(8,128)(2,1)}, u32[]{:S(2)}) copy-start(bf16[384,384]{1,0:T(8,128)(2,1)} %constant.26.clone.pack_hbm.pack_ref) | copy-start | bytes 884740
  4.4 24.4 %copy-start.1 = (bf16[128,3584]{1,0:T(8,128)(2,1)S(1)}, bf16[128,3584]{1,0:T(8,128)(2,1)}, u32[]{:S(2)}) copy-start(bf16[128,3584]{1,0:T(8,128)(2,1)} %og_ref) | copy-start | bytes 2752516
  4.5 55.5 %all-to-all-start = ((bf16[16,24,1792]{2,1,0:T(8,128)(2,1)}), bf16[16,24,1792]{2,1,0:T(8,128)(2,1)S(1)}, u32[]{:S(2)}, u32[]{:S(2)}) async-start(bf16[16,24,1792]{2,1,0:T(8,128)(2,1)} %bitcast.24), calls=%async_computation | async-start | bytes 2752512 | tf_op jit(solution)/shard_map/all_to_all | solution.py:265
  26.0 4.3 %collective-permute-start = (bf16[8,112,256]{2,1,0:T(8,128)(2,1)S(1)}, bf16[8,112,256]{2,1,0:T(8,128)(2,1)S(1)}, u32[]{:S(2)}, u32[]{:S(2)}) collective-permute-start(bf16[8,112,256]{2,1,0:T(8,128)(2,1)S(1)} %get-tuple-element.38), channel_id=1, source_target_pairs={{0,16},{16,0},{1,17},{17,1},{2,18},{18,2},{3,19},{19,3},{4,20},{20... | collective-permute-start | bytes 1376264 | tf_op jit(solution)/shard_map/ppermute | solution.py:305
  30.3 22.8 %collective-permute-start.1 = (bf16[224,256]{1,0:T(8,128)(2,1)S(1)}, bf16[224,256]{1,0:T(8,128)(2,1)S(1)}, u32[]{:S(2)}, u32[]{:S(2)}) collective-permute-start(bf16[224,256]{1,0:T(8,128)(2,1)S(1)} %get-tuple-element.44), channel_id=1, source_target_pairs={{0,128},{32,160},{64,192},{96,224},{128,0},{160,32},{192,64},{224,... | collective-permute-start | bytes 344072 | tf_op jit(solution)/shard_map/ppermute | solution.py:310
  37.5 18.0 %collective-permute-start.2 = (bf16[224,256]{1,0:T(8,128)(2,1)S(1)}, bf16[224,256]{1,0:T(8,128)(2,1)S(1)}, u32[]{:S(2)}, u32[]{:S(2)}) collective-permute-start(bf16[224,256]{1,0:T(8,128)(2,1)S(1)} %get-tuple-element.45), channel_id=1, source_target_pairs={{0,96},{32,128},{64,160},{96,192},{128,224},{160,0},{192,32},{224,... | collective-permute-start | bytes 344072 | tf_op jit(solution)/shard_map/ppermute | solution.py:310
  39.8 19.9 %collective-permute-start.3 = (bf16[224,256]{1,0:T(8,128)(2,1)S(1)}, bf16[224,256]{1,0:T(8,128)(2,1)S(1)}, u32[]{:S(2)}, u32[]{:S(2)}) collective-permute-start(bf16[224,256]{1,0:T(8,128)(2,1)S(1)} %get-tuple-element.46), channel_id=1, source_target_pairs={{0,160},{32,192},{64,224},{96,0},{128,32},{160,64},{192,96},{224,1... | collective-permute-start | bytes 344072 | tf_op jit(solution)/shard_map/ppermute | solution.py:310
  45.8 14.0 %collective-permute-start.4 = (bf16[224,256]{1,0:T(8,128)(2,1)S(1)}, bf16[224,256]{1,0:T(8,128)(2,1)S(1)}, u32[]{:S(2)}, u32[]{:S(2)}) collective-permute-start(bf16[224,256]{1,0:T(8,128)(2,1)S(1)} %get-tuple-element.47), channel_id=1, source_target_pairs={{0,64},{32,96},{64,128},{96,160},{128,192},{160,224},{192,0},{224,... | collective-permute-start | bytes 344072 | tf_op jit(solution)/shard_map/ppermute | solution.py:310
  48.0 11.7 %collective-permute-start.5 = (bf16[224,256]{1,0:T(8,128)(2,1)S(1)}, bf16[224,256]{1,0:T(8,128)(2,1)S(1)}, u32[]{:S(2)}, u32[]{:S(2)}) collective-permute-start(bf16[224,256]{1,0:T(8,128)(2,1)S(1)} %get-tuple-element.48), channel_id=1, source_target_pairs={{0,192},{32,224},{64,0},{96,32},{128,64},{160,96},{192,128},{224,1... | collective-permute-start | bytes 344072 | tf_op jit(solution)/shard_map/ppermute | solution.py:310
  53.2 6.7 %collective-permute-start.6 = (bf16[224,256]{1,0:T(8,128)(2,1)S(1)}, bf16[224,256]{1,0:T(8,128)(2,1)S(1)}, u32[]{:S(2)}, u32[]{:S(2)}) collective-permute-start(bf16[224,256]{1,0:T(8,128)(2,1)S(1)} %get-tuple-element.49), channel_id=1, source_target_pairs={{0,32},{32,64},{64,96},{96,128},{128,160},{160,192},{192,224},{224... | collective-permute-start | bytes 344072 | tf_op jit(solution)/shard_map/ppermute | solution.py:310
  55.4 12.0 %collective-permute-start.7 = (bf16[224,256]{1,0:T(8,128)(2,1)S(1)}, bf16[224,256]{1,0:T(8,128)(2,1)S(1)}, u32[]{:S(2)}, u32[]{:S(2)}) collective-permute-start(bf16[224,256]{1,0:T(8,128)(2,1)S(1)} %get-tuple-element.60), channel_id=1, source_target_pairs={{0,224},{32,0},{64,32},{96,64},{128,96},{160,128},{192,160},{224,1... | collective-permute-start | bytes 344072 | tf_op jit(solution)/shard_map/ppermute | solution.py:310
  61.3 13.2 %all-to-all-start.1 = ((f32[16,1,128]{2,1,0:T(1,128)}), f32[16,1,128]{2,1,0:T(1,128)S(1)}, u32[]{:S(2)}, u32[]{:S(2)}) async-start(f32[16,1,128]{2,1,0:T(1,128)} %get-tuple-element.52), calls=%async_computation.1 | async-start | bytes 16384 | tf_op jit(solution)/shard_map/all_to_all | solution.py:265
  76.5 23.8 %all-to-all-start.2 = ((bf16[64,8,128]{2,1,0:T(8,128)(2,1)}), bf16[64,8,128]{2,1,0:T(8,128)(2,1)S(1)}, u32[]{:S(2)}, u32[]{:S(2)}) async-start(bf16[64,8,128]{2,1,0:T(8,128)(2,1)} %contract.1), calls=%async_computation.2 | async-start | bytes 262144 | tf_op jit(solution)/shard_map/all_to_all | solution.py:265

commit v5 on v4

--- a/solution.py
+++ b/solution.py
@@ -23,7 +23,7 @@
 ROWS = SLOTS + META
 PEERS = 16
 RING = 8
-STEPS = (0, 4, 3, 5, 2, 6, 1, 7)
+STEPS = (0, 4, 5, 3, 7, 6, 2, 1)
 HELD = 7
 SCALE = 2.5
 
@@ -134,7 +134,7 @@
     gap = jnp.zeros((SLOTS, 64 - FEAT), bf16)
     x, core = place_ref[2], place_ref[3]
     for far_x in range(RING):
-        step = (far_x - x) & (RING - 1)
+        step = (far_x ^ x) & (RING - 1)
         pieces = []
         for k in (2 * far_x, 2 * far_x + 1):
             parts = []
@@ -193,7 +193,7 @@
         for o in range(2):
             at = o * ROWS + SLOTS
             meta = near_refs[n][at : at + META, :].astype(f32)
-            source = ((x - step) & (RING - 1)) * 2 + (core ^ o)
+            source = ((x ^ step) & (RING - 1)) * 2 + (core ^ o)
             term = jnp.zeros((EXPERTS, TOK), bf16)
             for k in range(TOPK):
                 coef = meta[k : k + 1, TOK:] + meta[8 + k : 9 + k, :TOK]
@@ -307,7 +307,7 @@
     joined = call(join, [((2 * ROWS, 256), bf16)] * RING, (own, other))
     near = [joined[0]]
     for step in STEPS[1:]:
-        near.append(lax.ppermute(joined[step], "x", [(i, (i + step) % RING) for i in range(RING)]))
+        near.append(lax.ppermute(joined[step], "x", [(i, i ^ step) for i in range(RING)]))
     got, og, *near[:HELD] = lax.optimization_barrier((got, og, *near[:HELD]))
     gates, send = call(
         gate, [((1, TOK), f32), ((PEERS, 1, TOK), f32)], (og, got, pack, idt, slots)

time: 102 us -> 103 us (level)
  waiting for transfers between devices: 17.4 us -> 20.3 us
  starting transfers between devices: 69.6 us -> 68.3 us
    ppermute x7, starting transfers between devices: 29.3 us -> 25.7 us  [shards(): lax.ppermute(joined[step], 'x', [(i, i ^ step) for i in range(RING)])]
    ppermute x7, waiting for transfers between devices: 0.21 us -> 3.2 us  [shards(): lax.ppermute(joined[step], 'x', [(i, i ^ step) for i in range(RING)])]
    all_to_all x3, starting transfers between devices: 37.5 us -> 39.7 us  [swap(): return lax.all_to_all(v, axes, split_axis=0, concat_axis=0, tiled=True)]
  transfers between devices with their start and end apart: 11 -> 11, of which waited for: 4 -> 6; matrix products, arithmetic and copies ran while one was open for 0% -> 0% of each run, Pallas kernels for 6% -> 6%
where the time goes in v5:
time: 103 us
  starting transfers between devices  68.3 us (66%)
  waiting for transfers between devices  20.3 us (20%)
  Pallas kernels  13 us (13%)
    all_to_all x3, starting transfers between devices, swap(): return lax.all_to_all(v, axes, split_axis=0, concat_axis=0, tiled=True)  39.7 us
    ppermute x7, starting transfers between devices, shards(): lax.ppermute(joined[step], 'x', [(i, i ^ step) for i in range(RING)])  25.7 us
    all_to_all x3, waiting for transfers between devices, swap(): return lax.all_to_all(v, axes, split_axis=0, concat_axis=0, tiled=True)  16.6 us
    pallas_call x8, Pallas kernels, call(): pl.pallas_call(body, out_shape=[jax.ShapeDtypeStruct(s, t) for s, t in ou...  13 us
    ppermute x7, waiting for transfers between devices, shards(): lax.ppermute(joined[step], 'x', [(i, i ^ step) for i in range(RING)])  3.2 us
    ppermute x1, starting transfers between devices, shards(): other = lax.ppermute(other, 'core', [(0, 1), (1, 0)])  2.87 us
  transfers between devices with their start and end apart: 11, of which 6 were waited for; matrix products, arithmetic and copies ran while one was open for 0% of the time, Pallas kernels for 6%

profile of v5, /device:TPU:1, one launch (start us, length us, event | category | flops | bytes accessed | tf_op | source)
XLA Modules:
  0.0 102.6 jit_solution(16969548619901162721)
XLA Ops:
  0.6 3.7 %outgoing.1 = (bf16[384,1792]{1,0:T(8,128)(2,1)}, bf16[96,3584]{1,0:T(8,128)(2,1)}) custom-call(s32[8,128]{1,0:T(8,128)} %bitcast.14, s32[1,128]{1,0:T(1,128)} %bitcast.19, bf16[128,3584]{1,0:T(8,128)(2,1)} %tv_hbm.1, bf16[28,128]{1,0:T(8,128)(2,1)} %bitcast.25, bf16[96,3584]{1,0:T(8,128)(2,1)} %eo_hbm.1, bf16[384,384]{1,0:T(8,128)(2,1)} %constant.26.clone.pack_hbm.pack_ref), custom_call_target="tpu_custom_call" | custom-call | tf_op jit(solution)/shard_map/outgoing/pallas_call | solution.py:253
  4.4 0.0 copy-start.3
  4.4 0.0 copy-start.4
  4.4 0.0 copy-start.5
  4.4 0.0 copy-start
  4.4 0.0 copy-start.1
  4.5 18.6 %all-to-all-start = ((bf16[16,24,1792]{2,1,0:T(8,128)(2,1)}), bf16[16,24,1792]{2,1,0:T(8,128)(2,1)S(1)}, u32[]{:S(2)}, u32[]{:S(2)}) async-start(bf16[16,24,1792]{2,1,0:T(8,128)(2,1)} %bitcast.24), calls=%async_computation | async-start | bytes 2752512 | tf_op jit(solution)/shard_map/all_to_all | solution.py:265
  23.1 0.1 copy.12.ids_ref
  23.2 0.1 pad_add_fusion.place_ref
  23.3 2.7 %prepare.1 = (bf16[8,112,256]{2,1,0:T(8,128)(2,1)S(1)}, bf16[8,112,256]{2,1,0:T(8,128)(2,1)S(1)}) custom-call(s32[4]{0:T(128)S(1)} %pad_add_fusion.place_ref, s32[8,128]{1,0:T(8,128)S(1)} %bitcast.15, s32[1,128]{1,0:T(1,128)S(1)} %bitcast.20, s32[128,8]{1,0:T(8,128)S(1)} %copy.12.ids_ref, f32[128,256]{1,0:T(8,128)S(1)} %copy-done.4, ...), custom_call_target="tpu_custom_call" | custom-call | tf_op jit(solution)/shard_map/prepare/pallas_call | solution.py:253
  26.0 2.9 %collective-permute-start = (bf16[8,112,256]{2,1,0:T(8,128)(2,1)S(1)}, bf16[8,112,256]{2,1,0:T(8,128)(2,1)S(1)}, u32[]{:S(2)}, u32[]{:S(2)}) collective-permute-start(bf16[8,112,256]{2,1,0:T(8,128)(2,1)S(1)} %get-tuple-element.38), channel_id=1, source_target_pairs={{0,16},{16,0},{1,17},{17,1},{2,18},{18,2},{3,19},{19,3},{4,20},{20... | collective-permute-start | bytes 1376264 | tf_op jit(solution)/shard_map/ppermute | solution.py:305
  28.9 0.8 grads.1.og_ref
  29.7 0.6 collective-permute-done.other_ref
  30.3 0.1 join.1
  30.3 7.1 %collective-permute-start.1 = (bf16[224,256]{1,0:T(8,128)(2,1)S(1)}, bf16[224,256]{1,0:T(8,128)(2,1)S(1)}, u32[]{:S(2)}, u32[]{:S(2)}) collective-permute-start(bf16[224,256]{1,0:T(8,128)(2,1)S(1)} %get-tuple-element.44), channel_id=1, source_target_pairs={{0,128},{32,160},{64,192},{96,224},{128,0},{160,32},{192,64},{224,... | collective-permute-start | bytes 344072 | tf_op jit(solution)/shard_map/ppermute | solution.py:310
  37.5 2.1 %collective-permute-start.2 = (bf16[224,256]{1,0:T(8,128)(2,1)S(1)}, bf16[224,256]{1,0:T(8,128)(2,1)S(1)}, u32[]{:S(2)}, u32[]{:S(2)}) collective-permute-start(bf16[224,256]{1,0:T(8,128)(2,1)S(1)} %get-tuple-element.45), channel_id=1, source_target_pairs={{0,160},{32,128},{64,224},{96,192},{128,32},{160,0},{192,96},{224,... | collective-permute-start | bytes 344072 | tf_op jit(solution)/shard_map/ppermute | solution.py:310
  39.6 4.0 %collective-permute-start.3 = (bf16[224,256]{1,0:T(8,128)(2,1)S(1)}, bf16[224,256]{1,0:T(8,128)(2,1)S(1)}, u32[]{:S(2)}, u32[]{:S(2)}) collective-permute-start(bf16[224,256]{1,0:T(8,128)(2,1)S(1)} %get-tuple-element.46), channel_id=1, source_target_pairs={{0,96},{32,64},{64,32},{96,0},{128,224},{160,192},{192,160},{224,1... | collective-permute-start | bytes 344072 | tf_op jit(solution)/shard_map/ppermute | solution.py:310
  43.6 4.4 %collective-permute-start.4 = (bf16[224,256]{1,0:T(8,128)(2,1)S(1)}, bf16[224,256]{1,0:T(8,128)(2,1)S(1)}, u32[]{:S(2)}, u32[]{:S(2)}) collective-permute-start(bf16[224,256]{1,0:T(8,128)(2,1)S(1)} %get-tuple-element.47), channel_id=1, source_target_pairs={{0,224},{32,192},{64,160},{96,128},{128,96},{160,64},{192,32},{224... | collective-permute-start | bytes 344072 | tf_op jit(solution)/shard_map/ppermute | solution.py:310
  48.0 3.0 %collective-permute-start.5 = (bf16[224,256]{1,0:T(8,128)(2,1)S(1)}, bf16[224,256]{1,0:T(8,128)(2,1)S(1)}, u32[]{:S(2)}, u32[]{:S(2)}) collective-permute-start(bf16[224,256]{1,0:T(8,128)(2,1)S(1)} %get-tuple-element.48), channel_id=1, source_target_pairs={{0,192},{32,224},{64,128},{96,160},{128,64},{160,96},{192,0},{224,... | collective-permute-start | bytes 344072 | tf_op jit(solution)/shard_map/ppermute | solution.py:310
  51.0 2.1 %collective-permute-start.6 = (bf16[224,256]{1,0:T(8,128)(2,1)S(1)}, bf16[224,256]{1,0:T(8,128)(2,1)S(1)}, u32[]{:S(2)}, u32[]{:S(2)}) collective-permute-start(bf16[224,256]{1,0:T(8,128)(2,1)S(1)} %get-tuple-element.49), channel_id=1, source_target_pairs={{0,64},{32,96},{64,0},{96,32},{128,192},{160,224},{192,128},{224,1... | collective-permute-start | bytes 344072 | tf_op jit(solution)/shard_map/ppermute | solution.py:310
  53.2 2.9 %collective-permute-start.7 = (bf16[224,256]{1,0:T(8,128)(2,1)S(1)}, bf16[224,256]{1,0:T(8,128)(2,1)S(1)}, u32[]{:S(2)}, u32[]{:S(2)}) collective-permute-start(bf16[224,256]{1,0:T(8,128)(2,1)S(1)} %get-tuple-element.60), channel_id=1, source_target_pairs={{0,32},{32,0},{64,96},{96,64},{128,160},{160,128},{192,224},{224,1... | collective-permute-start | bytes 344072 | tf_op jit(solution)/shard_map/ppermute | solution.py:310
  56.1 0.2 collective-permute-done.4.refs_4_
  56.3 2.6 %collective-permute-done.5.refs_5_ = bf16[224,256]{1,0:T(8,128)(2,1)S(1)} collective-permute-done((bf16[224,256]{1,0:T(8,128)(2,1)S(1)}, bf16[224,256]{1,0:T(8,128)(2,1)S(1)}, u32[]{:S(2)}, u32[]{:S(2)}) %collective-permute-start.5) | collective-permute-done | bytes 114720 | tf_op jit(solution)/shard_map/ppermute | solution.py:310
  58.9 0.4 collective-permute-done.6.refs_6_
  59.3 1.4 %gate.1 = (f32[1,128]{1,0:T(1,128)}, f32[16,1,128]{2,1,0:T(1,128)}) custom-call(bf16[384,896]{1,0:T(8,128)(2,1)S(1)} %grads.1.og_ref, bf16[384,1792]{1,0:T(8,128)(2,1)S(1)} %bitcast.12, bf16[384,384]{1,0:T(8,128)(2,1)S(1)} %copy-done, s32[8,128]{1,0:T(8,128)S(1)} %bitcast.17, s32[1,128]{1,0:T(1,128)S(1)} %bitcast.22), custom_call_target="tpu_custom_call" | custom-call | tf_op jit(solution)/shard_map/gate/pallas_call | solution.py:253
  60.6 8.4 %all-to-all-start.1 = ((f32[16,1,128]{2,1,0:T(1,128)}), f32[16,1,128]{2,1,0:T(1,128)S(1)}, u32[]{:S(2)}, u32[]{:S(2)}) async-start(f32[16,1,128]{2,1,0:T(1,128)} %get-tuple-element.52), calls=%async_computation.1 | async-start | bytes 16384 | tf_op jit(solution)/shard_map/all_to_all | solution.py:265
  69.1 6.9 %all-to-all-done.1.gg_ref = f32[16,1,128]{2,1,0:T(1,128)S(1)} async-done(((f32[16,1,128]{2,1,0:T(1,128)}), f32[16,1,128]{2,1,0:T(1,128)S(1)}, u32[]{:S(2)}, u32[]{:S(2)}) %all-to-all-start.1) | async-done | bytes 8224 | tf_op jit(solution)/shard_map/all_to_all | solution.py:265
  76.0 2.0 %contract.1 = bf16[64,8,128]{2,1,0:T(8,128)(2,1)} custom-call(s32[4]{0:T(128)S(1)} %pad_add_fusion.place_ref, f32[16,1,128]{2,1,0:T(1,128)S(1)} %all-to-all-done.1.gg_ref, s32[8,128]{1,0:T(8,128)S(1)} %bitcast.18, s32[1,128]{1,0:T(1,128)S(1)} %bitcast.23, bf16[224,256]{1,0:T(8,128)(2,1)S(1)} %get-tuple-element.53.refs_0_, ...), custom_call_target="tpu_custom_call" | custom-call | tf_op jit(solution)/shard_map/contract/pallas_call | solution.py:253
  78.1 12.7 %all-to-all-start.2 = ((bf16[64,8,128]{2,1,0:T(8,128)(2,1)}), bf16[64,8,128]{2,1,0:T(8,128)(2,1)S(1)}, u32[]{:S(2)}, u32[]{:S(2)}) async-start(bf16[64,8,128]{2,1,0:T(8,128)(2,1)} %contract.1), calls=%async_computation.2 | async-start | bytes 262144 | tf_op jit(solution)/shard_map/all_to_all | solution.py:265
  90.8 1.5 %unpack.1 = bf16[96,3584]{1,0:T(8,128)(2,1)} custom-call(bf16[384,1792]{1,0:T(8,128)(2,1)S(1)} %bitcast.13, bf16[384,384]{1,0:T(8,128)(2,1)S(1)} %copy-done), custom_call_target="tpu_custom_call" | custom-call | tf_op jit(solution)/shard_map/unpack/pallas_call | solution.py:253
  92.3 9.6 %all-to-all-done.2.far_ref = bf16[64,8,128]{2,1,0:T(8,128)(2,1)S(1)} async-done(((bf16[64,8,128]{2,1,0:T(8,128)(2,1)}), bf16[64,8,128]{2,1,0:T(8,128)(2,1)S(1)}, u32[]{:S(2)}, u32[]{:S(2)}) %all-to-all-start.2) | async-done | bytes 131104 | tf_op jit(solution)/shard_map/all_to_all | solution.py:265
  101.9 0.7 finish.1
  (12 shorter events, 0.0 us)
Async XLA Ops:
  4.4 18.7 %copy-start.3 = (s32[128,8]{0,1:T(8,128)S(1)}, s32[128,8]{0,1:T(8,128)}, u32[]{:S(2)}) copy-start(s32[128,8]{0,1:T(8,128)} %param.10) | copy-start | bytes 12292
  4.4 18.9 %copy-start.2 = (bf16[96,3584]{1,0:T(8,128)(2,1)S(1)}, bf16[96,3584]{1,0:T(8,128)(2,1)}, u32[]{:S(2)}) copy-start(bf16[96,3584]{1,0:T(8,128)(2,1)} %get-tuple-element.35.deq_ref) | copy-start | bytes 2064388
  4.4 18.9 %copy-start.4 = (f32[128,256]{1,0:T(8,128)S(1)}, f32[128,256]{1,0:T(8,128)}, u32[]{:S(2)}) copy-start(f32[128,256]{1,0:T(8,128)} %logits_ref.1) | copy-start | bytes 393220
  4.4 18.9 %copy-start.5 = (s32[128]{0:T(128)S(1)}, s32[128]{0:T(128)}, u32[]{:S(2)}) copy-start(s32[128]{0:T(128)} %param.11) | copy-start | bytes 1540
  4.4 24.4 %copy-start = (bf16[384,384]{1,0:T(8,128)(2,1)S(1)}, bf16[384,384]{1,0:T(8,128)(2,1)}, u32[]{:S(2)}) copy-start(bf16[384,384]{1,0:T(8,128)(2,1)} %constant.26.clone.pack_hbm.pack_ref) | copy-start | bytes 884740
  4.4 24.4 %copy-start.1 = (bf16[128,3584]{1,0:T(8,128)(2,1)S(1)}, bf16[128,3584]{1,0:T(8,128)(2,1)}, u32[]{:S(2)}) copy-start(bf16[128,3584]{1,0:T(8,128)(2,1)} %og_ref) | copy-start | bytes 2752516
  4.5 54.8 %all-to-all-start = ((bf16[16,24,1792]{2,1,0:T(8,128)(2,1)}), bf16[16,24,1792]{2,1,0:T(8,128)(2,1)S(1)}, u32[]{:S(2)}, u32[]{:S(2)}) async-start(bf16[16,24,1792]{2,1,0:T(8,128)(2,1)} %bitcast.24), calls=%async_computation | async-start | bytes 2752512 | tf_op jit(solution)/shard_map/all_to_all | solution.py:265
  26.0 4.3 %collective-permute-start = (bf16[8,112,256]{2,1,0:T(8,128)(2,1)S(1)}, bf16[8,112,256]{2,1,0:T(8,128)(2,1)S(1)}, u32[]{:S(2)}, u32[]{:S(2)}) collective-permute-start(bf16[8,112,256]{2,1,0:T(8,128)(2,1)S(1)} %get-tuple-element.38), channel_id=1, source_target_pairs={{0,16},{16,0},{1,17},{17,1},{2,18},{18,2},{3,19},{19,3},{4,20},{20... | collective-permute-start | bytes 1376264 | tf_op jit(solution)/shard_map/ppermute | solution.py:305
  30.3 20.7 %collective-permute-start.1 = (bf16[224,256]{1,0:T(8,128)(2,1)S(1)}, bf16[224,256]{1,0:T(8,128)(2,1)S(1)}, u32[]{:S(2)}, u32[]{:S(2)}) collective-permute-start(bf16[224,256]{1,0:T(8,128)(2,1)S(1)} %get-tuple-element.44), channel_id=1, source_target_pairs={{0,128},{32,160},{64,192},{96,224},{128,0},{160,32},{192,64},{224,... | collective-permute-start | bytes 344072 | tf_op jit(solution)/shard_map/ppermute | solution.py:310
  37.5 15.7 %collective-permute-start.2 = (bf16[224,256]{1,0:T(8,128)(2,1)S(1)}, bf16[224,256]{1,0:T(8,128)(2,1)S(1)}, u32[]{:S(2)}, u32[]{:S(2)}) collective-permute-start(bf16[224,256]{1,0:T(8,128)(2,1)S(1)} %get-tuple-element.45), channel_id=1, source_target_pairs={{0,160},{32,128},{64,224},{96,192},{128,32},{160,0},{192,96},{224,... | collective-permute-start | bytes 344072 | tf_op jit(solution)/shard_map/ppermute | solution.py:310
  39.6 16.5 %collective-permute-start.3 = (bf16[224,256]{1,0:T(8,128)(2,1)S(1)}, bf16[224,256]{1,0:T(8,128)(2,1)S(1)}, u32[]{:S(2)}, u32[]{:S(2)}) collective-permute-start(bf16[224,256]{1,0:T(8,128)(2,1)S(1)} %get-tuple-element.46), channel_id=1, source_target_pairs={{0,96},{32,64},{64,32},{96,0},{128,224},{160,192},{192,160},{224,1... | collective-permute-start | bytes 344072 | tf_op jit(solution)/shard_map/ppermute | solution.py:310
  43.6 12.7 %collective-permute-start.4 = (bf16[224,256]{1,0:T(8,128)(2,1)S(1)}, bf16[224,256]{1,0:T(8,128)(2,1)S(1)}, u32[]{:S(2)}, u32[]{:S(2)}) collective-permute-start(bf16[224,256]{1,0:T(8,128)(2,1)S(1)} %get-tuple-element.47), channel_id=1, source_target_pairs={{0,224},{32,192},{64,160},{96,128},{128,96},{160,64},{192,32},{224... | collective-permute-start | bytes 344072 | tf_op jit(solution)/shard_map/ppermute | solution.py:310
  48.0 10.9 %collective-permute-start.5 = (bf16[224,256]{1,0:T(8,128)(2,1)S(1)}, bf16[224,256]{1,0:T(8,128)(2,1)S(1)}, u32[]{:S(2)}, u32[]{:S(2)}) collective-permute-start(bf16[224,256]{1,0:T(8,128)(2,1)S(1)} %get-tuple-element.48), channel_id=1, source_target_pairs={{0,192},{32,224},{64,128},{96,160},{128,64},{160,96},{192,0},{224,... | collective-permute-start | bytes 344072 | tf_op jit(solution)/shard_map/ppermute | solution.py:310
  51.0 8.2 %collective-permute-start.6 = (bf16[224,256]{1,0:T(8,128)(2,1)S(1)}, bf16[224,256]{1,0:T(8,128)(2,1)S(1)}, u32[]{:S(2)}, u32[]{:S(2)}) collective-permute-start(bf16[224,256]{1,0:T(8,128)(2,1)S(1)} %get-tuple-element.49), channel_id=1, source_target_pairs={{0,64},{32,96},{64,0},{96,32},{128,192},{160,224},{192,128},{224,1... | collective-permute-start | bytes 344072 | tf_op jit(solution)/shard_map/ppermute | solution.py:310
  53.2 15.9 %collective-permute-start.7 = (bf16[224,256]{1,0:T(8,128)(2,1)S(1)}, bf16[224,256]{1,0:T(8,128)(2,1)S(1)}, u32[]{:S(2)}, u32[]{:S(2)}) collective-permute-start(bf16[224,256]{1,0:T(8,128)(2,1)S(1)} %get-tuple-element.60), channel_id=1, source_target_pairs={{0,32},{32,0},{64,96},{96,64},{128,160},{160,128},{192,224},{224,1... | collective-permute-start | bytes 344072 | tf_op jit(solution)/shard_map/ppermute | solution.py:310
  60.6 15.4 %all-to-all-start.1 = ((f32[16,1,128]{2,1,0:T(1,128)}), f32[16,1,128]{2,1,0:T(1,128)S(1)}, u32[]{:S(2)}, u32[]{:S(2)}) async-start(f32[16,1,128]{2,1,0:T(1,128)} %get-tuple-element.52), calls=%async_computation.1 | async-start | bytes 16384 | tf_op jit(solution)/shard_map/all_to_all | solution.py:265
  78.1 23.8 %all-to-all-start.2 = ((bf16[64,8,128]{2,1,0:T(8,128)(2,1)}), bf16[64,8,128]{2,1,0:T(8,128)(2,1)S(1)}, u32[]{:S(2)}, u32[]{:S(2)}) async-start(bf16[64,8,128]{2,1,0:T(8,128)(2,1)} %contract.1), calls=%async_computation.2 | async-start | bytes 262144 | tf_op jit(solution)/shard_map/all_to_all | solution.py:265
